TPU v7x, 128 devices: a whole 4x4x4 slice. The times are simulated.
128 devices in a mesh: pb: 16 (over y, x), ga: 8 (over z, core).
Axes of the slice: x: 4, y: 4, z: 4, core: 2. Of those that a mesh axis runs over, the one named last changes fastest.
Arguments:
- irr_vectors: bfloat16 [8, 16384, 2048], P(None, ('pb', 'ga')), may hold values from -0.046875 to 0.046875
- inv_dielectric: bfloat16 [16, 2048, 2048], P('pb', 'ga'), may hold values from -0.125 to 0.125
- pair_density: bfloat16 [16, 16384, 512], P('pb', 'ga'), may hold values from -6 to 6
- minus_q: int32 [16], replicated, may hold values from 0 to 15, as said below
- sym_op: int32 [16], replicated, may hold values from 0 to 47
- rot_blocks: int32 [48, 128], replicated, may hold values from 0 to 127, as said below
- rot_rows: int32 [48, 128, 128], replicated, may hold values from 0 to 127, each once within a row
- phase_bits: int32 [48, 16384], replicated, may hold values 0 or 1
Outputs:
- screened_density: bfloat16 [16, 16384, 512], P('pb', 'ga')
Inputs may be any that keep to these rules, and one draw needn't show every extreme that they name: minus_q pairs the q-points: minus_q[minus_q[q]] = q and minus_q[q] != q. Each row rot_blocks[o] is a permutation of the 128 blocks; among the 16 destination blocks a * 16 to a * 16 + 15 of any slab a, at most 3 have source blocks with one value of the source block index mod 8, and every slab of every operation reaches 3 for some value.
All inputs are finite; a program needn't handle non-finite values.
Results may differ from a plain program's by a relative error of at most 0.0056.
Values may be sent and summed in bfloat16 or wider, within the bound.
A program may use at most 128 MiB of HBM per device.

v0:
```python
import math

import jax
import jax.numpy as jnp
import numpy as np
from jax import lax
from jax.sharding import PartitionSpec as P


def selector(mate):

    def pick(total, piece, start):
        chosen = jnp.arange(piece.shape[0], dtype=jnp.int32) == mate
        kept = jnp.where(chosen[:, None, None], piece, jnp.zeros((), piece.dtype))
        return jnp.sum(kept, axis=0)

    return pick


def on_device(
    irr_vectors, inv_dielectric, pair_density, minus_q, sym_op, rot_blocks, rot_rows, phase_bits
):
    q_count = lax.axis_size("pb")
    g_count = lax.axis_size("ga")
    owner = lax.axis_index("pb")
    slab_index = lax.axis_index("ga")
    irr_count, block_rows, width = irr_vectors.shape
    blocks_all = q_count * g_count
    capacity = q_count // g_count + 1
    slab_rows = q_count * block_rows
    basis_rows = width // g_count
    ratio = math.sqrt(slab_rows * g_count / width)
    table = jnp.take(rot_blocks, sym_op, axis=0)
    source_ga = table % g_count
    places = jnp.arange(blocks_all, dtype=jnp.int32)
    earlier = (places[None, :] < places[:, None]) & (
        places[None, :] // q_count == places[:, None] // q_count
    )
    ranks = jnp.sum(
        (earlier[None] & (source_ga[:, None, :] == source_ga[:, :, None])).astype(jnp.int32), axis=2
    )
    own_table = lax.dynamic_index_in_dim(table, owner, 0, keepdims=False)
    own_ranks = lax.dynamic_index_in_dim(ranks, owner, 0, keepdims=False)
    which_irr = np.arange(q_count) % irr_count
    outgoing = irr_vectors[which_irr]
    arrived = lax.all_to_all(outgoing, "pb", split_axis=0, concat_axis=0, tiled=True)
    senders = jnp.arange(q_count, dtype=jnp.int32) * g_count + slab_index
    match = own_table[None, :] == senders[:, None]
    dest_block = jnp.sum(jnp.where(match, places[None, :], 0), axis=1)
    dest_rank = jnp.sum(jnp.where(match, own_ranks[None, :], 0), axis=1)
    slot_of = dest_block // q_count * capacity + dest_rank
    slots = jnp.arange(g_count * capacity, dtype=jnp.int32)
    hits = slots[:, None] == slot_of[None, :]
    source_of = jnp.sum(jnp.where(hits, jnp.arange(q_count, dtype=jnp.int32)[None, :], 0), axis=1)
    filled = jnp.any(hits, axis=1)
    operation = lax.dynamic_index_in_dim(sym_op, owner, 0, keepdims=False)
    mine_source = lax.dynamic_slice_in_dim(own_table, slab_index * q_count, q_count)
    mine_rank = lax.dynamic_slice_in_dim(own_ranks, slab_index * q_count, q_count)
    row_table = lax.dynamic_slice_in_dim(
        lax.dynamic_index_in_dim(rot_rows, operation, 0, keepdims=False),
        slab_index * q_count,
        q_count,
    )
    bits = lax.dynamic_slice_in_dim(
        lax.dynamic_index_in_dim(phase_bits, operation, 0, keepdims=False),
        slab_index * slab_rows,
        slab_rows,
    )
    signs = (1 - 2 * bits).astype(jnp.bfloat16)
    send_slot = mine_source % g_count * capacity + mine_rank
    packed = jnp.where(
        filled[:, None, None], jnp.take(arrived, source_of, axis=0), jnp.zeros((), jnp.bfloat16)
    )
    packed = packed.reshape(g_count, capacity, block_rows, width)
    received = lax.all_to_all(packed, "ga", split_axis=0, concat_axis=0, tiled=True)
    row_index = (send_slot * block_rows)[:, None] + row_table
    vectors = jnp.take(received.reshape(-1, width), row_index.reshape(-1), axis=0)
    vectors = vectors * signs[:, None]
    partial_value = jnp.einsum(
        "gb,gp->bp", vectors, pair_density[0], preferred_element_type=jnp.float32
    )
    coef = lax.psum(partial_value, "ga").astype(jnp.bfloat16)
    rows_own = inv_dielectric[0]
    own_term = jnp.dot(rows_own, coef, preferred_element_type=jnp.float32)
    coef_rows = lax.dynamic_slice_in_dim(coef, slab_index * basis_rows, basis_rows)
    mate = lax.dynamic_index_in_dim(minus_q, owner, 0, keepdims=False)
    pick = selector(mate)
    empty_rows = jnp.zeros(rows_own.shape, jnp.bfloat16)
    mate_rows = pick(
        empty_rows, lax.all_gather(inv_dielectric, "pb", axis=0, tiled=True), jnp.int32(0)
    )
    mate_cols = lax.all_to_all(mate_rows, "ga", split_axis=1, concat_axis=0, tiled=True)
    other_term = jnp.einsum("bc,bp->cp", mate_cols, coef, preferred_element_type=jnp.float32)
    screened = (0.5 * (own_term + other_term) - coef_rows.astype(jnp.float32)).astype(jnp.bfloat16)
    whole = lax.all_gather(screened, "ga", axis=0, tiled=True)
    result = (jnp.dot(vectors, whole, preferred_element_type=jnp.float32) * ratio).astype(
        jnp.bfloat16
    )
    return result[None]


def solution(mesh):
    in_specs = (
        P(None, ("pb", "ga"), None),
        P("pb", "ga", None),
        P("pb", "ga", None),
        P(),
        P(),
        P(),
        P(),
        P(),
    )
    out_specs = P("pb", "ga", None)
    return jax.shard_map(
        on_device, mesh=mesh, in_specs=in_specs, out_specs=out_specs, check_vma=False
    )
```

profile of v0, /device:TPU:1, one launch (start us, length us, event | category | flops | bytes accessed | tf_op | source)
XLA Modules:
  0.0 506.7 jit_solution(13661814611086551963)
XLA Ops:
  6.5 0.7 all-gather.3.cloned.1.call-update
  7.3 0.7 pad_clamp_fusion.1
  7.9 6.7 %gather_fusion.1 = bf16[16,128,2048]{2,1,0:T(8,128)(2,1)} fusion(bf16[8,128,2048]{2,1,0:T(8,128)(2,1)} %param.10, s32[1024]{0:T(1024)S(1)} %pad_clamp_fusion.1), kind=kCustom, calls=%fused_computation.1 | custom fusion | bytes 16777280 | tf_op jit(solution)/shard_map/gather | solution.py:45
  14.6 7.8 %all-to-all-start = ((bf16[16,128,2048]{2,1,0:T(8,128)(2,1)}), bf16[16,128,2048]{2,1,0:T(8,128)(2,1)}, u32[]{:S(2)}, u32[]{:S(2)}) async-start(bf16[16,128,2048]{2,1,0:T(8,128)(2,1)} %gather_fusion.1), calls=%async_computation | async-start | bytes 16777216 | tf_op jit(solution)/shard_map/all_to_all | solution.py:46
  22.4 0.6 gather_fusion
  23.2 0.6 convert_reduce_fusion
  23.9 0.2 fusion.8
  24.0 0.1 multiply_add_fusion
  24.1 0.1 fusion.11
  24.2 0.1 broadcast_in_dim.119
  24.3 0.1 select_reduce_fusion.1
  24.5 149.4 %all-to-all-done = bf16[16,128,2048]{2,1,0:T(8,128)(2,1)} async-done(((bf16[16,128,2048]{2,1,0:T(8,128)(2,1)}), bf16[16,128,2048]{2,1,0:T(8,128)(2,1)}, u32[]{:S(2)}, u32[]{:S(2)}) %all-to-all-start) | async-done | bytes 8388640 | tf_op jit(solution)/shard_map/all_to_all | solution.py:46
  173.9 9.8 %gather_fusion.2 = bf16[24,128,2048]{2,1,0:T(8,128)(2,1)} fusion(bf16[16,128,2048]{2,1,0:T(8,128)(2,1)} %all-to-all-done, s32[1024]{0:T(1024)S(1)} %pad_clamp_fusion), kind=kCustom, calls=%fused_computation.2 | custom fusion | bytes 25165920 | tf_op jit(solution)/shard_map/jit(_take)/gather | solution.py:72
  183.7 10.9 %select_select_fusion = bf16[8,3,128,2048]{3,2,1,0:T(8,128)(2,1)} fusion(bf16[8,3,128,2048]{3,2,1,0:T(8,128)(2,1)} %bitcast.50, pred[8,3]{1,0:T(8,128)(4,1)S(1)} %compare_and_fusion.1, pred[8,3]{1,0:T(8,128)(4,1)S(1)} %broadcast_in_dim.119), kind=kLoop, calls=%fused_computation.5 | loop fusion | flops 12582912 | bytes 25165872 | tf_op jit(solution)/shard_map/jit(_where)/select_n | solution.py:71
  194.6 12.9 %all-to-all-start.1 = ((bf16[8,3,128,2048]{3,2,1,0:T(8,128)(2,1)}), bf16[8,3,128,2048]{3,2,1,0:T(8,128)(2,1)}, u32[]{:S(2)}, u32[]{:S(2)}) async-start(bf16[8,3,128,2048]{3,2,1,0:T(8,128)(2,1)} %select_select_fusion), calls=%async_computation.1 | async-start | bytes 25165824 | tf_op jit(solution)/shard_map/all_to_all | solution.py:75
  207.6 0.6 dynamic_slice.45
  209.5 0.6 dynamic_slice.52
  210.7 1.0 convert_reduce_fusion.1
  211.7 0.6 iota_compare_fusion.2
  212.2 0.8 compare_and_fusion
  213.1 133.2 %all-to-all-done.1 = bf16[8,3,128,2048]{3,2,1,0:T(8,128)(2,1)} async-done(((bf16[8,3,128,2048]{3,2,1,0:T(8,128)(2,1)}), bf16[8,3,128,2048]{3,2,1,0:T(8,128)(2,1)}, u32[]{:S(2)}, u32[]{:S(2)}) %all-to-all-start.1) | async-done | bytes 12582944 | tf_op jit(solution)/shard_map/all_to_all | solution.py:75
  346.4 22.5 %gather_fusion.3 = bf16[2048,2048]{1,0:T(8,128)(2,1)} fusion(bf16[3072,2048]{1,0:T(8,128)(2,1)} %bitcast.10, s32[2048]{0:T(1024)S(1)} %broadcast_clamp_fusion), kind=kCustom, calls=%fused_computation.3 | custom fusion | bytes 16785408 | tf_op jit(solution)/shard_map/jit(_take)/gather | solution.py:77
  368.9 10.2 %fusion.1 = f32[2048,512]{1,0:T(8,128)} fusion(bf16[1,2048,512]{2,1,0:T(8,128)(2,1)S(1)} %copy-done, bf16[2048,2048]{1,0:T(8,128)(2,1)} %gather_fusion.3, pred[2048]{0:T(1024)(128)(4,1)S(1)} %get-tuple-element.7, bf16[2048]{0:T(1024)(128)(2,1)S(1)} %convert_reduce_fusion.1), kind=kOutput, calls=%fused_computation.9 | convolution fusion | flops 4303355904 | bytes 14686208 | tf_op jit(solution)/shard_map/gb,gp->bp/dot_general | solution.py:79
  379.1 10.1 %select_reduce_fusion = bf16[256,2048]{1,0:T(8,128)(2,1)S(1)} fusion(bf16[16,256,2048]{2,1,0:T(8,128)(2,1)} %all-gather.3.cloned.1.call-done, pred[16]{0:T(512)(128)(4,1)S(1)} %iota_compare_fusion.2), kind=kLoop, calls=%fused_computation.4 | loop fusion | flops 16252928 | bytes 17825808 | tf_op jit(solution)/shard_map/reduce_sum | solution.py:15
  389.2 1.3 copy.17
  390.5 4.3 all-to-all-start.2
  394.9 64.0 %all-reduce.1 = bf16[2048,512]{1,0:T(8,128)(2,1)} all-reduce(f32[2048,512]{1,0:T(8,128)} %fusion.1), channel_id=1, replica_groups=mesh['pb'=16,'ga'=8] {'ga'}, use_global_device_ids=true, to_apply=%region_5.6 | all-reduce | flops 1048576 | bytes 6291456 | tf_op jit(solution)/shard_map/psum | solution.py:82
  458.8 3.4 convolution_bitcast_fusion
  462.3 1.3 copy.18
  463.6 3.5 fusion.5
  467.1 24.1 %all-gather.5.cloned.1.call-done = bf16[2048,512]{1,0:T(8,128)(2,1)} async-done(((bf16[256,512]{1,0:T(8,128)(2,1)}), bf16[2048,512]{1,0:T(8,128)(2,1)}) %all-gather.5.cloned.1.call-update) | async-done | bytes 2097168 | tf_op jit(solution)/shard_map/all_gather | solution.py:95
  491.3 8.6 %fusion = bf16[1,2048,512]{2,1,0:T(8,128)(2,1)} fusion(bf16[2048,512]{1,0:T(8,128)(2,1)} %all-gather.5.cloned.1.call-done, bf16[2048,2048]{1,0:T(8,128)(2,1)} %gather_fusion.3, pred[2048]{0:T(1024)(128)(4,1)S(1)} %get-tuple-element.7, bf16[2048]{0:T(1024)(128)(2,1)S(1)} %convert_reduce_fusion.1), kind=kOutput, calls=%fused_computation.8 | convolution fusion | flops 4305453056 | bytes 12589056 | tf_op jit(solution)/shard_map/dot_general | solution.py:96
  (29 shorter events, 0.4 us)
Async XLA Ops:
  6.5 362.4 %copy-start = (bf16[1,2048,512]{2,1,0:T(8,128)(2,1)S(1)}, bf16[1,2048,512]{2,1,0:T(8,128)(2,1)}, u32[]{:S(2)}) copy-start(bf16[1,2048,512]{2,1,0:T(8,128)(2,1)} %param.12) | copy-start | bytes 6291460
  6.5 372.6 %all-gather.3.cloned.1.call-start = ((), (), s32[]{:S(2)}) async-start(), calls=%async_computation.3 | async-start | bytes 17825792 | tf_op jit(solution)/shard_map/all_gather | solution.py:90
  14.6 7.8 %copy-start.2 = (s32[16]{0:T(128)S(1)}, s32[16]{0:T(128)}, u32[]{:S(2)}) copy-start(s32[16]{0:T(128)} %param.14) | copy-start | bytes 196
  14.6 7.8 %copy-start.1 = (s32[48,128]{1,0:T(8,128)S(1)}, s32[48,128]{1,0:T(8,128)}, u32[]{:S(2)}) copy-start(s32[48,128]{1,0:T(8,128)} %param.15) | copy-start | bytes 73732
  14.6 159.3 %all-to-all-start = ((bf16[16,128,2048]{2,1,0:T(8,128)(2,1)}), bf16[16,128,2048]{2,1,0:T(8,128)(2,1)}, u32[]{:S(2)}, u32[]{:S(2)}) async-start(bf16[16,128,2048]{2,1,0:T(8,128)(2,1)} %gather_fusion.1), calls=%async_computation | async-start | bytes 16777216 | tf_op jit(solution)/shard_map/all_to_all | solution.py:46
  194.6 14.8 %copy-start.3 = (s32[16]{0:T(128)S(1)}, s32[16]{0:T(128)}, u32[]{:S(2)}) copy-start(s32[16]{0:T(128)} %param.13) | copy-start | bytes 196
  194.6 151.7 %all-to-all-start.1 = ((bf16[8,3,128,2048]{3,2,1,0:T(8,128)(2,1)}), bf16[8,3,128,2048]{3,2,1,0:T(8,128)(2,1)}, u32[]{:S(2)}, u32[]{:S(2)}) async-start(bf16[8,3,128,2048]{3,2,1,0:T(8,128)(2,1)} %select_select_fusion), calls=%async_computation.1 | async-start | bytes 25165824 | tf_op jit(solution)/shard_map/all_to_all | solution.py:75
  390.5 71.7 %all-to-all-start.2 = ((bf16[256,8,256]{0,2,1:T(8,128)(2,1)}), bf16[256,8,256]{0,2,1:T(8,128)(2,1)S(1)}, u32[]{:S(2)}, u32[]{:S(2)}) async-start(bf16[256,8,256]{0,2,1:T(8,128)(2,1)} %bitcast.52), calls=%async_computation.2 | async-start | bytes 2097152 | tf_op jit(solution)/shard_map/all_to_all | solution.py:92
  394.9 96.4 %all-gather.5.cloned.1.call-start = ((), (), s32[]{:S(2)}) async-start(), calls=%async_computation.4 | async-start | bytes 2359296 | tf_op jit(solution)/shard_map/all_gather | solution.py:95
Sparse Core Ops, SparseCore 0:
  9.5 215.9 all-gather.2
  467.2 23.9 all-gather.4
where the time goes:
time: 508 us; the launch traced here: 507 us
  waiting for transfers between devices  307 us (60%)
  blocking collectives  64 us (13%)
  local copies, waits for them, and re-layouts  43.6 us (9%)
  matrix products  25.8 us (5%)
  other arithmetic  25.4 us (5%)
  starting transfers between devices  25 us (5%)
  between operations  15.5 us (3%)
    all_to_all x1, waiting for transfers between devices, on_device(): lax.all_to_all(outgoing, 'pb', split_axis=0, concat_axis=0, tiled=True)  149 us
    all_to_all x1, waiting for transfers between devices, on_device(): lax.all_to_all(packed, 'ga', split_axis=0, concat_axis=0, tiled=True)  133 us
    psum x1, blocking collectives, on_device(): coef = lax.psum(partial_value, 'ga').astype(jnp.bfloat16)  64 us
    all_gather x1, waiting for transfers between devices, on_device(): whole = lax.all_gather(screened, 'ga', axis=0, tiled=True)  24.1 us
    gather x1, local copies, waits for them, and re-layouts, on_device(): jnp.take(received.reshape(-1, width), row_index.reshape(-1), axis=0)  22.5 us
    all_to_all x1, starting transfers between devices, on_device(): lax.all_to_all(packed, 'ga', split_axis=0, concat_axis=0, tiled=True)  12.9 us
    select_n x1, other arithmetic, on_device(): jnp.where(filled[:, None, None], jnp.take(arrived, source_of, axis=0), jn...  10.9 us
    dot_general x1, matrix products, on_device(): jnp.einsum('gb,gp->bp', vectors, pair_density[0], preferred_element_type=...  10.2 us
  transfers between devices with their start and end apart: 5, of which 3 were waited for; matrix products, arithmetic and copies ran while one was open for 14% of the time, Pallas kernels for 0%

commit v1 on v0

v1 whole, which is shorter than its diff:
```python
import math

import jax
import jax.numpy as jnp
from jax import lax
from jax.experimental import pallas as pl
from jax.experimental.pallas import tpu as pltpu
from jax.sharding import PartitionSpec as P

MESH = pl.DeviceIdType.MESH
NX = 4
NC = 2
SEMS = 200
CAP = 3
BF16 = jnp.bfloat16
F32 = jnp.float32


def dot_nt(a, b):
    return lax.dot_general(a, b, (((1,), (1,)), ((), ())), preferred_element_type=F32)


def kernel(
    ratio,
    irr,
    dmat,
    drows,
    density,
    row_table,
    bits,
    minus_q,
    block_of_slot,
    held_slot,
    held_of_slot,
    send_slot,
    out,
    held,
    fwd,
    via_x,
    rho_tx,
    rho_rx_low,
    rho_rx_high,
    rho_group,
    part_tx,
    part_rx,
    acc,
    acc2,
    core_rx,
    core_rx2,
    sum_tx,
    sum_tx2,
    sum_rx,
    sum_rx2,
    mate_sum,
    coef,
    slab_sum,
    own_d,
    spread,
    chosen,
    mate_rows,
    mate_cols,
    screened,
    mate_scr,
    res_low,
    res_high,
    mate_res,
    back_low,
    back_high,
    turn_back,
    local_sem,
    send_sem,
    recv_sem,
):
    q_count = lax.axis_size("pb")
    g_count = lax.axis_size("ga")
    pb = lax.axis_index("pb")
    ga = lax.axis_index("ga")
    y, x = pb // NX, pb % NX
    z, c = ga // NC, ga % NC
    z_count = g_count // NC
    sibling = z * NC + (1 - c)
    basis = own_d.shape[0]
    rows = row_table.shape[1]
    plus, minus, beyond = (lambda v: (v + 1) % NX), (lambda v: (v + 3) % NX), (lambda v: (v + 2) % NX)
    ahead, behind = (lambda v: (v + 1 + 2 * c) % NX), (lambda v: (v + 3 - 2 * c) % NX)
    up, down, across = plus(y), minus(y), beyond(y)
    parts = range(2)
    res = (res_low, res_high)
    rho_rx = (rho_rx_low, rho_rx_high)
    back = (back_low, back_high)
    wide = res_low.shape[1]
    started = []
    taken = [0]

    def sems(count):
        first = taken[0]
        taken[0] += count
        assert taken[0] <= SEMS
        return first

    def copy(src, dst, i, to):
        return pltpu.make_async_remote_copy(
            src_ref=src,
            dst_ref=dst,
            send_sem=send_sem.at[i],
            recv_sem=recv_sem.at[i],
            device_id=to,
            device_id_type=MESH,
        )

    def send(src, dst, i, to):
        one = copy(src, dst, i, to)
        one.start()
        started.append(one)

    def arrive(dst, i):
        copy(dst, dst, i, (pb, ga)).wait_recv()

    def on_x(t):
        return (y * NX + t, ga)

    def on_y(t):
        return (t * NX + x, ga)

    class Exchange:
        def __init__(self, me, to, src, dst, via):
            self.me, self.to, self.src, self.dst, self.via = me, to, src, dst, via
            self.i = sems(4)

        def start(self):
            me = self.me
            send(self.src(plus(me)), self.dst(me), self.i, self.to(plus(me)))
            send(self.src(minus(me)), self.dst(me), self.i + 1, self.to(minus(me)))
            send(self.src(beyond(me)), self.via, self.i + 2, self.to(ahead(me)))

        def forward(self):
            arrive(self.via, self.i + 2)
            send(self.via, self.dst(behind(self.me)), self.i + 3, self.to(ahead(self.me)))

        def from_minus(self):
            arrive(self.dst(minus(self.me)), self.i)

        def from_plus(self):
            arrive(self.dst(plus(self.me)), self.i + 1)

        def from_beyond(self):
            arrive(self.dst(beyond(self.me)), self.i + 3)

        def finish(self):
            self.from_minus()
            self.from_plus()
            self.from_beyond()

    load_rho = pltpu.make_async_copy(density, out, local_sem.at[0])
    load_rho.start()

    barrier = pltpu.get_barrier_semaphore()

    def greet_pb(d, carry):
        pl.semaphore_signal(
            barrier, inc=1, device_id=((pb + d) % q_count, ga), device_id_type=MESH
        )
        return carry

    def greet_ga(d, carry):
        pl.semaphore_signal(
            barrier, inc=1, device_id=(pb, (ga + d) % g_count), device_id_type=MESH
        )
        return carry

    lax.fori_loop(1, q_count, greet_pb, 0)
    lax.fori_loop(1, g_count, greet_ga, 0)
    pl.semaphore_wait(barrier, q_count + g_count - 2)

    own_irr = NX * (y % 2)
    next_irr = NX * ((y + 1) % 2)
    next_x = Exchange(x, on_x, lambda t: irr.at[next_irr + t], lambda s: fwd.at[s], via_x.at[0])
    own_x = Exchange(x, on_x, lambda t: irr.at[own_irr + t], lambda s: held.at[y, s], via_x.at[1])
    next_x.start()
    keep = pltpu.make_async_copy(irr.at[own_irr + x], held.at[y, x], local_sem.at[1])
    keep.start()
    y_sem = sems(8)

    def to_neighbours(k, source, src):
        there = held.at[y, source]
        send(src, there, y_sem + k, on_y(up))
        send(src, there, y_sem + 4 + k, on_y(down))

    to_neighbours(0, x, irr.at[next_irr + x])

    def turn_of(j):
        sources = lax.broadcasted_iota(jnp.int32, (rows, rows), 0)
        sign = (1 - 2 * bits[pl.ds(j, 1), :]).astype(F32)
        return jnp.where(row_table[pl.ds(j, 1), :] == sources, sign, 0.0)

    load_rho.wait()
    rho_sem = sems(2 * g_count)

    def rho_copy(h, d):
        to = (ga + d) % g_count
        return copy(
            rho_tx.at[h, pl.ds(to * CAP, CAP)],
            rho_rx[h].at[pl.ds(ga * CAP, CAP)],
            rho_sem + h * g_count + d,
            (pb, to),
        )

    for h in parts:

        def make_turned(j, carry):
            value = jnp.dot(
                turn_of(j).astype(BF16),
                out[j, :, h * wide : (h + 1) * wide],
                preferred_element_type=F32,
            )
            res[h][j] = value.astype(BF16).T
            return carry

        def rho_start(k, carry):
            d = (k + 2) % (g_count - 1) + 1
            to = (ga + d) % g_count
            for i in range(CAP):
                rho_tx[h, to * CAP + i] = res[h][block_of_slot[to * CAP + i]]
            rho_copy(h, d).start()
            return carry

        lax.fori_loop(0, q_count, make_turned, 0)
        lax.fori_loop(0, g_count - 1, rho_start, 0)
        for i in range(CAP):
            rho_rx[h][ga * CAP + i] = res[h][block_of_slot[ga * CAP + i]]

    load_d = pltpu.make_async_copy(drows, own_d, local_sem.at[3])
    load_d.start()

    next_x.from_minus()
    to_neighbours(1, minus(x), fwd.at[minus(x)])
    next_x.from_plus()
    to_neighbours(2, plus(x), fwd.at[plus(x)])
    next_x.forward()
    own_x.start()

    d1_sem, d2_sem = sems(q_count), sems(q_count)

    def spread_copy(d):
        to = (pb + d) % q_count
        return copy(dmat.at[to], spread.at[pb], d1_sem + d, (to, ga))

    def spread_start(d, carry):
        spread_copy(d).start()
        return carry

    lax.fori_loop(1, q_count, spread_start, 0)
    keep_d1 = pltpu.make_async_copy(dmat.at[pb], spread.at[pb], local_sem.at[2])
    keep_d1.start()

    def make_turn_back(j, carry):
        turn_back[j] = turn_of(j).T.astype(BF16)
        return carry

    lax.fori_loop(0, q_count, make_turn_back, 0)
    next_x.from_beyond()
    to_neighbours(3, beyond(x), fwd.at[beyond(x)])
    own_x.forward()

    def group(h, row):
        return jnp.concatenate([rho_rx[h][held_slot[row * NX + i]] for i in range(NX)], axis=1)

    def project(row, values, total, first):
        def one(n, carry):
            columns = pl.ds(pl.multiple_of(n * basis, basis), basis)
            block = held[row, :, :, columns].reshape(-1, basis)
            part = jnp.dot(values[...], block, preferred_element_type=F32)
            total[n] = part if first else total[n] + part
            return carry

        lax.fori_loop(0, g_count, one, 0)

    part_sem = sems(4)
    for h in parts:

        def rho_wait(d, carry):
            source = (ga + g_count - d) % g_count
            arrive(rho_rx[h].at[pl.ds(source * CAP, CAP)], rho_sem + h * g_count + d)
            return carry

        lax.fori_loop(1, g_count, rho_wait, 0)
        part_tx[h] = group(h, across)
        send(part_tx.at[h], part_rx.at[h], part_sem + h, on_y(across))

    def spread_wait(d, carry):
        arrive(spread.at[(pb + q_count - d) % q_count], d1_sem + d)
        return carry

    lax.fori_loop(1, q_count, spread_wait, 0)
    keep_d1.wait()

    def choose(q, carry):
        chosen[q] = spread[minus_q[q]]
        return carry

    lax.fori_loop(0, q_count, choose, 0)

    def mate_copy(d):
        to = (pb + d) % q_count
        return copy(chosen.at[to], mate_rows.at[pb], d2_sem + d, (to, ga))

    def mate_start(d, carry):
        mate_copy(d).start()
        return carry

    lax.fori_loop(1, q_count, mate_start, 0)
    keep_d2 = pltpu.make_async_copy(chosen.at[pb], mate_rows.at[pb], local_sem.at[2])
    keep_d2.start()

    class Reduce:
        def __init__(self, total, landing, outgoing, incoming):
            self.total, self.landing = total, landing
            self.outgoing, self.incoming = outgoing, incoming
            self.i = sems(2 * z_count)

        def to_core(self, k):
            return copy(
                self.total.at[k * NC + (1 - c)], self.landing.at[k], self.i + k, (pb, sibling)
            )

        def start(self):
            for k in range(z_count):
                self.to_core(k).start()

        def sent(self):
            for k in range(z_count):
                self.to_core(k).wait_send()

        def along_z(self):
            for d in (2, 1, 3):
                k = (z + d) % z_count
                arrive(self.landing.at[k], self.i + k)
                self.outgoing[d] = (self.total[k * NC + c] + self.landing[k]).astype(BF16)
                send(
                    self.outgoing.at[d],
                    self.incoming.at[d],
                    self.i + z_count + d,
                    (pb, k * NC + c),
                )
            arrive(self.landing.at[z], self.i + z)

        def finish(self):
            value = self.total[ga] + self.landing[z]
            for d in (1, 3, 2):
                arrive(self.incoming.at[d], self.i + z_count + d)
                value = value + self.incoming[d].astype(F32)
            return value

    reduce1 = [Reduce(acc.at[h], core_rx.at[h], sum_tx.at[h], sum_rx.at[h]) for h in parts]
    reduce2 = [Reduce(acc2.at[h], core_rx2.at[h], sum_tx2.at[h], sum_rx2.at[h]) for h in parts]

    own_x.finish()
    keep.wait()
    for h in parts:
        arrive(part_rx.at[h], part_sem + h)
        project(y, part_rx.at[h], acc2.at[h], True)
        reduce2[h].start()
    for h in parts:
        rho_group[...] = group(h, y)
        project(y, rho_group, acc.at[h], True)
        reduce2[h].along_z()
    for k, s in enumerate((x, minus(x), plus(x), beyond(x))):
        arrive(held.at[down, s], y_sem + k)
        arrive(held.at[up, s], y_sem + 4 + k)
    for h in parts:
        for row in (down, up):
            rho_group[...] = group(h, row)
            project(row, rho_group, acc.at[h], False)
        reduce1[h].start()
    for h in parts:
        mate_sum[h, 0] = reduce2[h].finish().astype(BF16)
        send(mate_sum.at[h, 0], mate_sum.at[h, 1], part_sem + 2 + h, on_y(across))
        reduce1[h].along_z()

    def mate_wait(d, carry):
        arrive(mate_rows.at[(pb + q_count - d) % q_count], d2_sem + d)
        return carry

    lax.fori_loop(1, q_count, mate_wait, 0)
    keep_d2.wait()

    column_sem = sems(g_count)

    def column_copy(d):
        to = (ga + d) % g_count
        columns = pl.ds(pl.multiple_of(to * basis, basis), basis)
        return copy(mate_rows.at[:, :, columns], mate_cols.at[ga], column_sem + d, (pb, to))

    def column_start(d, carry):
        column_copy(d).start()
        return carry

    lax.fori_loop(1, g_count, column_start, 0)
    own_columns = pl.ds(pl.multiple_of(ga * basis, basis), basis)
    keep_cols = pltpu.make_async_copy(
        mate_rows.at[:, :, own_columns], mate_cols.at[ga], local_sem.at[4]
    )
    keep_cols.start()

    class Gather:
        def __init__(self, ref, use):
            self.ref, self.use = ref, use
            self.i = sems(8)

        def start(self):
            mine = self.ref.at[ga]
            for d in (2, 1, 3):
                send(mine, mine, self.i + d, (pb, (z + d) % z_count * NC + c))
            send(mine, mine, self.i, (pb, sibling))

        def own(self):
            self.use(ga)

        def beside(self):
            arrive(self.ref.at[sibling], self.i)
            self.use(sibling)

        def along_z(self):
            for d in (1, 3, 2):
                source = (z + z_count - d) % z_count * NC + c
                there = self.ref.at[source]
                arrive(there, self.i + d)
                send(there, there, self.i + 4 + d, (pb, sibling))
                self.use(source)

        def rest(self):
            for d in (1, 3, 2):
                source = (z + z_count - d) % z_count * NC + (1 - c)
                arrive(self.ref.at[source], self.i + 4 + d)
                self.use(source)

    def column_wait(d, carry):
        arrive(mate_cols.at[(ga + g_count - d) % g_count], column_sem + d)
        return carry

    def apply(h):
        def use(n):
            columns = pl.ds(pl.multiple_of(n * basis, basis), basis)
            other = jnp.dot(
                coef[h, n], mate_cols[n].reshape(basis, basis), preferred_element_type=F32
            )
            slab_sum[h] += dot_nt(coef[h, n], own_d[:, columns]) + other

        return use

    gather_coef = [Gather(coef.at[h], apply(h)) for h in parts]
    for h in parts:
        value = reduce1[h].finish()
        arrive(mate_sum.at[h, 1], part_sem + 2 + h)
        coef[h, ga] = (value + mate_sum[h, 1].astype(F32)).astype(BF16)
        gather_coef[h].start()
    lax.fori_loop(1, g_count, column_wait, 0)
    keep_cols.wait()
    load_d.wait()
    slab_sum[...] = jnp.zeros_like(slab_sum)

    half = NX // 2

    def part_of(k):
        return (y + NX - 1 + k // 2) % NX, k % 2

    def expand(values, total, first_part, count):
        first = [True]

        def use(n):
            columns = pl.ds(pl.multiple_of(n * basis, basis), basis)
            fresh = first.pop() if first else False

            def one(k, carry):
                row, side = part_of(first_part + k)
                block = held[row, pl.ds(side * half, half), :, columns].reshape(-1, basis)
                value = dot_nt(values[n], block)
                total[k] = value if fresh else total[k] + value
                return carry

            lax.fori_loop(0, count, one, 0)

        return use

    mate_sem = sems(4)
    gather_own, gather_mate = [], []
    for h in parts:
        gather_own.append(
            Gather(screened.at[h], expand(screened.at[h], acc2.at[h], 0, 2 * (NX - 1)))
        )
        gather_mate.append(Gather(mate_scr.at[h], expand(mate_scr.at[h], acc.at[h], 2, 2)))
    for h in parts:
        gather_coef[h].own()
        gather_coef[h].beside()
    for h in parts:
        gather_coef[h].along_z()
        gather_coef[h].rest()
        screened[h, ga] = (0.5 * slab_sum[h] - coef[h, ga].astype(F32)).astype(BF16)
        send(screened.at[h, ga], mate_scr.at[h, ga], mate_sem + h, on_y(across))
        gather_own[h].start()
    for h in parts:
        reduce1[h].sent()
        reduce2[h].sent()
    for h in parts:
        gather_own[h].own()
        arrive(mate_scr.at[h, ga], mate_sem + h)
        gather_mate[h].start()

    def rho_sent(d, carry):
        for h in parts:
            rho_copy(h, d).wait_send()
        return carry

    lax.fori_loop(1, g_count, rho_sent, 0)
    back_sem = sems(2 * g_count)

    def back_copy(h, d):
        to = (ga + d) % g_count
        return copy(
            rho_tx.at[h, pl.ds(to * CAP, CAP)],
            back[h].at[pl.ds(ga * CAP, CAP)],
            back_sem + h * g_count + d,
            (pb, to),
        )

    for h in parts:
        gather_own[h].beside()
        gather_own[h].along_z()
        gather_mate[h].own()
        gather_mate[h].beside()
        gather_mate[h].along_z()
        gather_mate[h].rest()
        for k in range(2):
            value = (acc[h, k] * ratio).astype(BF16)
            for i in range(half):
                mate_res[h, k * half + i] = value[:, i * rows : (i + 1) * rows]
        send(mate_res.at[h], res[h].at[pl.ds(y * NX, NX)], mate_sem + 2 + h, on_y(across))
        gather_own[h].rest()

        def finish_rows(k, carry):
            row, side = part_of(k)
            value = (acc2[h, k] * ratio).astype(BF16)
            for i in range(half):
                res[h][row * NX + side * half + i] = value[:, i * rows : (i + 1) * rows]
            return carry

        lax.fori_loop(0, 2 * (NX - 1), finish_rows, 0)
        arrive(res[h].at[pl.ds(across * NX, NX)], mate_sem + 2 + h)

        def back_start(k, carry):
            d = (k + 2) % (g_count - 1) + 1
            to = (ga + d) % g_count
            for i in range(CAP):
                rho_tx[h, to * CAP + i] = res[h][held_of_slot[to * CAP + i]]
            back_copy(h, d).start()
            return carry

        lax.fori_loop(0, g_count - 1, back_start, 0)
        for i in range(CAP):
            back[h][ga * CAP + i] = res[h][held_of_slot[ga * CAP + i]]

    for h in parts:

        def back_wait(d, carry):
            source = (ga + g_count - d) % g_count
            arrive(back[h].at[pl.ds(source * CAP, CAP)], back_sem + h * g_count + d)
            return carry

        def unturn(j, carry):
            value = dot_nt(turn_back[j], back[h][send_slot[j]])
            out[j, :, h * wide : (h + 1) * wide] = value.astype(BF16)
            return carry

        lax.fori_loop(1, g_count, back_wait, 0)
        lax.fori_loop(0, q_count, unturn, 0)

    for one in started:
        one.wait_send()

    def drain_pb(d, carry):
        spread_copy(d).wait_send()
        mate_copy(d).wait_send()
        return carry

    def drain_ga(d, carry):
        column_copy(d).wait_send()
        for h in parts:
            back_copy(h, d).wait_send()
        return carry

    lax.fori_loop(1, q_count, drain_pb, 0)
    lax.fori_loop(1, g_count, drain_ga, 0)


def on_device(
    irr_vectors, inv_dielectric, pair_density, minus_q, sym_op, rot_blocks, rot_rows, phase_bits
):
    q_count = lax.axis_size("pb")
    g_count = lax.axis_size("ga")
    owner = lax.axis_index("pb")
    slab_index = lax.axis_index("ga")
    irr_count, block_rows, width = irr_vectors.shape
    density_width = pair_density.shape[2]
    blocks_all = q_count * g_count
    slab_rows = q_count * block_rows
    basis_rows = width // g_count
    slot_count = g_count * CAP
    ratio = math.sqrt(slab_rows * g_count / width)

    operation = lax.dynamic_index_in_dim(sym_op, owner, 0, keepdims=False)
    table = lax.dynamic_index_in_dim(rot_blocks, operation, 0, keepdims=False)
    places = jnp.arange(blocks_all, dtype=jnp.int32)
    source_ga = table % g_count
    earlier = (places[None, :] < places[:, None]) & (
        places[None, :] // q_count == places[:, None] // q_count
    )
    ranks = jnp.sum(
        (earlier & (source_ga[None, :] == source_ga[:, None])).astype(jnp.int32), axis=1
    )
    mine_source = lax.dynamic_slice_in_dim(table, slab_index * q_count, q_count)
    mine_rank = lax.dynamic_slice_in_dim(ranks, slab_index * q_count, q_count)
    send_slot = mine_source % g_count * CAP + mine_rank
    slots = jnp.arange(slot_count, dtype=jnp.int32)
    local = jnp.arange(q_count, dtype=jnp.int32)
    block_of_slot = jnp.sum(
        jnp.where(slots[:, None] == send_slot[None, :], local[None, :], 0), axis=1
    )
    senders = local * g_count + slab_index
    match = table[None, :] == senders[:, None]
    dest_block = jnp.sum(jnp.where(match, places[None, :], 0), axis=1)
    dest_rank = jnp.sum(jnp.where(match, ranks[None, :], 0), axis=1)
    held_slot = dest_block // q_count * CAP + dest_rank
    held_of_slot = jnp.sum(
        jnp.where(slots[:, None] == held_slot[None, :], local[None, :], 0), axis=1
    )

    row_table = lax.dynamic_slice_in_dim(
        lax.dynamic_index_in_dim(rot_rows, operation, 0, keepdims=False),
        slab_index * q_count,
        q_count,
    )
    bits = lax.dynamic_slice_in_dim(
        lax.dynamic_index_in_dim(phase_bits, operation, 0, keepdims=False),
        slab_index * slab_rows,
        slab_rows,
    ).reshape(q_count, block_rows)

    vmem = pltpu.VMEM
    dma = pltpu.SemaphoreType.DMA
    wide = density_width // 2
    slab = (wide, basis_rows)
    slots = (slot_count, wide, block_rows)
    chunk = basis_rows // q_count
    any_spec = pl.BlockSpec(memory_space=pl.ANY)
    smem_spec = pl.BlockSpec(memory_space=pltpu.SMEM)
    vmem_spec = pl.BlockSpec(memory_space=pltpu.VMEM)

    def run(*operands):
        return pl.pallas_call(
            lambda *refs: kernel(ratio, *refs),
            out_shape=jax.ShapeDtypeStruct((q_count, block_rows, density_width), BF16),
            in_specs=[any_spec] * 4 + [vmem_spec] * 2 + [smem_spec] * 5,
            out_specs=vmem_spec,
            scratch_shapes=[
                vmem((NX, NX, block_rows, width), BF16),
                vmem((NX, block_rows, width), BF16),
                vmem((2, block_rows, width), BF16),
                vmem((2, *slots), BF16),
                vmem(slots, BF16),
                vmem(slots, BF16),
                vmem((wide, NX * block_rows), BF16),
                vmem((2, wide, NX * block_rows), BF16),
                vmem((2, wide, NX * block_rows), BF16),
                vmem((2, g_count, *slab), F32),
                vmem((2, g_count, *slab), F32),
                vmem((2, g_count // NC, *slab), F32),
                vmem((2, g_count // NC, *slab), F32),
                vmem((2, g_count // NC, *slab), BF16),
                vmem((2, g_count // NC, *slab), BF16),
                vmem((2, g_count // NC, *slab), BF16),
                vmem((2, g_count // NC, *slab), BF16),
                vmem((2, 2, *slab), BF16),
                vmem((2, g_count, *slab), BF16),
                vmem((2, *slab), F32),
                vmem((basis_rows, width), BF16),
                vmem((q_count, chunk, width), BF16),
                vmem((q_count, chunk, width), BF16),
                vmem((q_count, chunk, width), BF16),
                vmem((g_count, q_count, chunk, basis_rows), BF16),
                vmem((2, g_count, *slab), BF16),
                vmem((2, g_count, *slab), BF16),
                vmem((q_count, wide, block_rows), BF16),
                vmem((q_count, wide, block_rows), BF16),
                vmem((2, NX, wide, block_rows), BF16),
                vmem(slots, BF16),
                vmem(slots, BF16),
                vmem((q_count, block_rows, block_rows), BF16),
                dma((5,)),
                dma((SEMS,)),
                dma((SEMS,)),
            ],
            compiler_params=pltpu.CompilerParams(
                collective_id=0, has_side_effects=True, vmem_limit_bytes=62 * 1024 * 1024
            ),
        )(*operands)

    out = run(
        irr_vectors,
        inv_dielectric[0].reshape(q_count, chunk, width),
        inv_dielectric[0],
        pair_density[0].reshape(q_count, block_rows, density_width),
        row_table,
        bits,
        minus_q,
        block_of_slot,
        held_slot,
        held_of_slot,
        send_slot,
    )
    return out.reshape(1, slab_rows, density_width)


def solution(mesh):
    in_specs = (
        P(None, ("pb", "ga"), None),
        P("pb", "ga", None),
        P("pb", "ga", None),
        P(),
        P(),
        P(),
        P(),
        P(),
    )
    out_specs = P("pb", "ga", None)
    return jax.shard_map(
        on_device, mesh=mesh, in_specs=in_specs, out_specs=out_specs, check_vma=False
    )
```

time: 508 us -> 226 us (0.44)
  waiting for transfers between devices: 307 us -> 0 us
  Pallas kernels: 0 us -> 213 us
  blocking collectives: 64 us -> 0 us
  local copies, waits for them, and re-layouts: 43.6 us -> 7.16 us
  matrix products: 25.8 us -> 0 us
  starting transfers between devices: 25 us -> 0 us
  other arithmetic: 25.4 us -> 3.75 us
  between operations: 15.5 us -> 1.97 us
    all_to_all x3 -> x0, waiting for transfers between devices: 283 us -> none  [the longest x1 149 us: on_device(): lax.all_to_all(outgoing, 'pb', split_axis=0, concat_axis=0, tiled=True)]
    pallas_call x0 -> x1, Pallas kernels: none -> 213 us  [run(): pl.pallas_call(lambda *refs: kernel(ratio, *refs), out_shape=jax.ShapeDty...]
    psum x1 -> x0, blocking collectives: 64 us -> none  [on_device(): coef = lax.psum(partial_value, 'ga').astype(jnp.bfloat16)]
    gather x4 -> x0, local copies, waits for them, and re-layouts: 39.6 us -> none  [the longest x1 22.5 us: on_device(): jnp.take(received.reshape(-1, width), row_index.reshape(-1), axis=0)]
    dot_general x4 -> x0, matrix products: 25.8 us -> none  [the longest x1 10.2 us: on_device(): jnp.einsum('gb,gp->bp', vectors, pair_density[0], preferred_element_type=...]
    all_to_all x3 -> x0, starting transfers between devices: 25 us -> none  [the longest x1 12.9 us: on_device(): lax.all_to_all(packed, 'ga', split_axis=0, concat_axis=0, tiled=True)]
    all_gather x2 -> x0, waiting for transfers between devices: 24.1 us -> none  [the longest x1 24.1 us: on_device(): whole = lax.all_gather(screened, 'ga', axis=0, tiled=True)]
    select_n x5 -> x0, other arithmetic: 11 us -> none  [the longest x1 10.9 us: on_device(): jnp.where(filled[:, None, None], jnp.take(arrived, source_of, axis=0), jn...]
  transfers between devices with their start and end apart: 5 -> 0, of which waited for: 3 -> 0; matrix products, arithmetic and copies ran while one was open for 14% -> 0% of each run, Pallas kernels for 0% -> 0%
where the time goes in v1:
time: 226 us
  Pallas kernels  213 us (94%)
  local copies, waits for them, and re-layouts  7.16 us (3%)
  other arithmetic  3.75 us (2%)
    pallas_call x1, Pallas kernels, run(): pl.pallas_call(lambda *refs: kernel(ratio, *refs), out_shape=jax.ShapeDty...  213 us

profile of v1, /device:TPU:1, one launch (start us, length us, event | category | flops | bytes accessed | tf_op | source)
XLA Modules:
  0.0 226.0 jit_solution(9560423861294585673)
XLA Ops:
  0.0 1.2 dynamic_slice.28
  3.2 0.7 fusion.6
  3.9 0.7 and_select_fusion.1
  4.6 0.2 convert_reduce_fusion
  4.8 0.8 fusion.5.refs_10_
  5.5 0.0 copy-start
  5.5 0.2 fusion.2
  5.7 0.0 copy-start.1
  5.8 0.6 select_reduce_fusion.refs_9_
  6.3 0.6 select_reduce_fusion.1.refs_7_
  7.0 1.3 dynamic-slice_bitcast_fusion.refs_4_
  8.3 1.6 dynamic_slice.31
  9.8 0.0 copy-done
  9.8 0.0 copy-done.1
  9.8 213.1 %shard_map.82 = bf16[16,128,512]{2,1,0:T(8,128)(2,1)} custom-call(bf16[8,128,2048]{2,1,0:T(8,128)(2,1)} %refs_0_.1, bf16[16,16,2048]{2,1,0:T(8,128)(2,1)} %bitcast.16, bf16[256,2048]{1,0:T(8,128)(2,1)} %bitcast.17, bf16[16,128,512]{2,1,0:T(8,128)(2,1)} %bitcast.18, s32[16,128]{1,0:T(8,128)} %dynamic-slice_bitcast_fusion.refs_4_, s32[16,128]{1,0:T(8,128)} %bitcast.19, ...), custom_call_target="tpu_custom_call" | custom-call | tf_op jit(solution)/shard_map/pallas_call | solution.py:659
  223.0 3.0 %copy.10 = bf16[1,2048,512]{2,1,0:T(8,128)(2,1)} copy(bf16[1,2048,512]{2,1,0:T(8,128)(2,1)} %bitcast.15) | data formatting | bytes 4194304
  (2 shorter events, 0.0 us)
Async XLA Ops:
  5.5 4.3 %copy-start = (s32[16]{0:T(128)}, s32[16]{0:T(128)S(1)}, u32[]{:S(2)}) copy-start(s32[16]{0:T(128)S(1)} %fusion.5.refs_10_) | copy-start | bytes 196
  5.7 4.1 %copy-start.1 = (s32[16]{0:T(128)}, s32[16]{0:T(128)S(1)}, u32[]{:S(2)}) copy-start(s32[16]{0:T(128)S(1)} %multiply_add_fusion.refs_8_) | copy-start | bytes 196

commit v2 on v1

--- a/solution.py
+++ b/solution.py
@@ -14,10 +14,6 @@
 CAP = 3
 BF16 = jnp.bfloat16
 F32 = jnp.float32
-
-
-def dot_nt(a, b):
-    return lax.dot_general(a, b, (((1,), (1,)), ((), ())), preferred_element_type=F32)
 
 
 def kernel(
@@ -59,6 +55,7 @@
     chosen,
     mate_rows,
     mate_cols,
+    mate_t,
     screened,
     mate_scr,
     res_low,
@@ -88,7 +85,7 @@
     res = (res_low, res_high)
     rho_rx = (rho_rx_low, rho_rx_high)
     back = (back_low, back_high)
-    wide = res_low.shape[1]
+    wide = res_low.shape[2]
     started = []
     taken = [0]
 
@@ -213,7 +210,7 @@
                 out[j, :, h * wide : (h + 1) * wide],
                 preferred_element_type=F32,
             )
-            res[h][j] = value.astype(BF16).T
+            res[h][j] = value.astype(BF16)
             return carry
 
         def rho_start(k, carry):
@@ -239,20 +236,6 @@
     next_x.forward()
     own_x.start()
 
-    d1_sem, d2_sem = sems(q_count), sems(q_count)
-
-    def spread_copy(d):
-        to = (pb + d) % q_count
-        return copy(dmat.at[to], spread.at[pb], d1_sem + d, (to, ga))
-
-    def spread_start(d, carry):
-        spread_copy(d).start()
-        return carry
-
-    lax.fori_loop(1, q_count, spread_start, 0)
-    keep_d1 = pltpu.make_async_copy(dmat.at[pb], spread.at[pb], local_sem.at[2])
-    keep_d1.start()
-
     def make_turn_back(j, carry):
         turn_back[j] = turn_of(j).T.astype(BF16)
         return carry
@@ -263,7 +246,7 @@
     own_x.forward()
 
     def group(h, row):
-        return jnp.concatenate([rho_rx[h][held_slot[row * NX + i]] for i in range(NX)], axis=1)
+        return jnp.concatenate([rho_rx[h][held_slot[row * NX + i]] for i in range(NX)], axis=0).T
 
     def project(row, values, total, first):
         def one(n, carry):
@@ -286,31 +269,6 @@
         lax.fori_loop(1, g_count, rho_wait, 0)
         part_tx[h] = group(h, across)
         send(part_tx.at[h], part_rx.at[h], part_sem + h, on_y(across))
-
-    def spread_wait(d, carry):
-        arrive(spread.at[(pb + q_count - d) % q_count], d1_sem + d)
-        return carry
-
-    lax.fori_loop(1, q_count, spread_wait, 0)
-    keep_d1.wait()
-
-    def choose(q, carry):
-        chosen[q] = spread[minus_q[q]]
-        return carry
-
-    lax.fori_loop(0, q_count, choose, 0)
-
-    def mate_copy(d):
-        to = (pb + d) % q_count
-        return copy(chosen.at[to], mate_rows.at[pb], d2_sem + d, (to, ga))
-
-    def mate_start(d, carry):
-        mate_copy(d).start()
-        return carry
-
-    lax.fori_loop(1, q_count, mate_start, 0)
-    keep_d2 = pltpu.make_async_copy(chosen.at[pb], mate_rows.at[pb], local_sem.at[2])
-    keep_d2.start()
 
     class Reduce:
         def __init__(self, total, landing, outgoing, incoming):
@@ -356,6 +314,20 @@
 
     own_x.finish()
     keep.wait()
+    d1_sem, d2_sem = sems(q_count), sems(q_count)
+
+    def spread_copy(d):
+        to = (pb + d) % q_count
+        return copy(dmat.at[to], spread.at[pb], d1_sem + d, (to, ga))
+
+    def spread_start(d, carry):
+        spread_copy(d).start()
+        return carry
+
+    lax.fori_loop(1, q_count, spread_start, 0)
+    keep_d1 = pltpu.make_async_copy(dmat.at[pb], spread.at[pb], local_sem.at[2])
+    keep_d1.start()
+
     for h in parts:
         arrive(part_rx.at[h], part_sem + h)
         project(y, part_rx.at[h], acc2.at[h], True)
@@ -367,6 +339,31 @@
     for k, s in enumerate((x, minus(x), plus(x), beyond(x))):
         arrive(held.at[down, s], y_sem + k)
         arrive(held.at[up, s], y_sem + 4 + k)
+    def spread_wait(d, carry):
+        arrive(spread.at[(pb + q_count - d) % q_count], d1_sem + d)
+        return carry
+
+    lax.fori_loop(1, q_count, spread_wait, 0)
+    keep_d1.wait()
+
+    def choose(q, carry):
+        chosen[q] = spread[minus_q[q]]
+        return carry
+
+    lax.fori_loop(0, q_count, choose, 0)
+
+    def mate_copy(d):
+        to = (pb + d) % q_count
+        return copy(chosen.at[to], mate_rows.at[pb], d2_sem + d, (to, ga))
+
+    def mate_start(d, carry):
+        mate_copy(d).start()
+        return carry
+
+    lax.fori_loop(1, q_count, mate_start, 0)
+    keep_d2 = pltpu.make_async_copy(chosen.at[pb], mate_rows.at[pb], local_sem.at[2])
+    keep_d2.start()
+
     for h in parts:
         for row in (down, up):
             rho_group[...] = group(h, row)
@@ -441,10 +438,9 @@
     def apply(h):
         def use(n):
             columns = pl.ds(pl.multiple_of(n * basis, basis), basis)
-            other = jnp.dot(
-                coef[h, n], mate_cols[n].reshape(basis, basis), preferred_element_type=F32
-            )
-            slab_sum[h] += dot_nt(coef[h, n], own_d[:, columns]) + other
+            slab_sum[h] += jnp.dot(
+                own_d[:, columns], coef[h, n], preferred_element_type=F32
+            ) + jnp.dot(mate_t[:, columns], coef[h, n], preferred_element_type=F32)
 
         return use
 
@@ -452,19 +448,26 @@
     for h in parts:
         value = reduce1[h].finish()
         arrive(mate_sum.at[h, 1], part_sem + 2 + h)
-        coef[h, ga] = (value + mate_sum[h, 1].astype(F32)).astype(BF16)
+        coef[h, ga] = (value + mate_sum[h, 1].astype(F32)).astype(BF16).T
         gather_coef[h].start()
     lax.fori_loop(1, g_count, column_wait, 0)
     keep_cols.wait()
     load_d.wait()
+
+    def turn_columns(n, carry):
+        columns = pl.ds(pl.multiple_of(n * basis, basis), basis)
+        mate_t[:, columns] = mate_cols[n].reshape(basis, basis).T
+        return carry
+
+    lax.fori_loop(0, g_count, turn_columns, 0)
     slab_sum[...] = jnp.zeros_like(slab_sum)
 
     half = NX // 2
 
-    def part_of(k):
-        return (y + NX - 1 + k // 2) % NX, k % 2
-
-    def expand(values, total, first_part, count):
+    def row_of(k):
+        return (y + NX - 1 + k) % NX
+
+    def expand(values, total, first_row, count):
         first = [True]
 
         def use(n):
@@ -472,10 +475,11 @@
             fresh = first.pop() if first else False
 
             def one(k, carry):
-                row, side = part_of(first_part + k)
-                block = held[row, pl.ds(side * half, half), :, columns].reshape(-1, basis)
-                value = dot_nt(values[n], block)
-                total[k] = value if fresh else total[k] + value
+                block = held[row_of(first_row + k), :, :, columns].reshape(-1, basis)
+                value = jnp.dot(block, values[n], preferred_element_type=F32)
+                value = value.reshape(half, -1, wide)
+                place = pl.ds(k * half, half)
+                total[place] = value if fresh else total[place] + value
                 return carry
 
             lax.fori_loop(0, count, one, 0)
@@ -486,9 +490,9 @@
     gather_own, gather_mate = [], []
     for h in parts:
         gather_own.append(
-            Gather(screened.at[h], expand(screened.at[h], acc2.at[h], 0, 2 * (NX - 1)))
+            Gather(screened.at[h], expand(screened.at[h], acc2.at[h], 0, NX - 1))
         )
-        gather_mate.append(Gather(mate_scr.at[h], expand(mate_scr.at[h], acc.at[h], 2, 2)))
+        gather_mate.append(Gather(mate_scr.at[h], expand(mate_scr.at[h], acc.at[h], 1, 1)))
     for h in parts:
         gather_coef[h].own()
         gather_coef[h].beside()
@@ -530,21 +534,16 @@
         gather_mate[h].beside()
         gather_mate[h].along_z()
         gather_mate[h].rest()
-        for k in range(2):
-            value = (acc[h, k] * ratio).astype(BF16)
-            for i in range(half):
-                mate_res[h, k * half + i] = value[:, i * rows : (i + 1) * rows]
+        mate_res[h] = (acc[h, :half] * ratio).astype(BF16).reshape(NX, rows, wide)
         send(mate_res.at[h], res[h].at[pl.ds(y * NX, NX)], mate_sem + 2 + h, on_y(across))
         gather_own[h].rest()
 
         def finish_rows(k, carry):
-            row, side = part_of(k)
-            value = (acc2[h, k] * ratio).astype(BF16)
-            for i in range(half):
-                res[h][row * NX + side * half + i] = value[:, i * rows : (i + 1) * rows]
+            value = (acc2[h, pl.ds(k * half, half)] * ratio).astype(BF16)
+            res[h][pl.ds(row_of(k) * NX, NX)] = value.reshape(NX, rows, wide)
             return carry
 
-        lax.fori_loop(0, 2 * (NX - 1), finish_rows, 0)
+        lax.fori_loop(0, NX - 1, finish_rows, 0)
         arrive(res[h].at[pl.ds(across * NX, NX)], mate_sem + 2 + h)
 
         def back_start(k, carry):
@@ -567,7 +566,7 @@
             return carry
 
         def unturn(j, carry):
-            value = dot_nt(turn_back[j], back[h][send_slot[j]])
+            value = jnp.dot(turn_back[j], back[h][send_slot[j]], preferred_element_type=F32)
             out[j, :, h * wide : (h + 1) * wide] = value.astype(BF16)
             return carry
 
@@ -649,7 +648,8 @@
     dma = pltpu.SemaphoreType.DMA
     wide = density_width // 2
     slab = (wide, basis_rows)
-    slots = (slot_count, wide, block_rows)
+    square = (basis_rows, wide)
+    slots = (slot_count, block_rows, wide)
     chunk = basis_rows // q_count
     any_spec = pl.BlockSpec(memory_space=pl.ANY)
     smem_spec = pl.BlockSpec(memory_space=pltpu.SMEM)
@@ -680,18 +680,19 @@
                 vmem((2, g_count // NC, *slab), BF16),
                 vmem((2, g_count // NC, *slab), BF16),
                 vmem((2, 2, *slab), BF16),
-                vmem((2, g_count, *slab), BF16),
-                vmem((2, *slab), F32),
+                vmem((2, g_count, *square), BF16),
+                vmem((2, *square), F32),
                 vmem((basis_rows, width), BF16),
                 vmem((q_count, chunk, width), BF16),
                 vmem((q_count, chunk, width), BF16),
                 vmem((q_count, chunk, width), BF16),
                 vmem((g_count, q_count, chunk, basis_rows), BF16),
-                vmem((2, g_count, *slab), BF16),
-                vmem((2, g_count, *slab), BF16),
-                vmem((q_count, wide, block_rows), BF16),
-                vmem((q_count, wide, block_rows), BF16),
-                vmem((2, NX, wide, block_rows), BF16),
+                vmem((basis_rows, width), BF16),
+                vmem((2, g_count, *square), BF16),
+                vmem((2, g_count, *square), BF16),
+                vmem((q_count, block_rows, wide), BF16),
+                vmem((q_count, block_rows, wide), BF16),
+                vmem((2, NX, block_rows, wide), BF16),
                 vmem(slots, BF16),
                 vmem(slots, BF16),
                 vmem((q_count, block_rows, block_rows), BF16),

time: 226 us -> 213 us (0.942)
  Pallas kernels: 213 us -> 200 us
    pallas_call x1, Pallas kernels: 213 us -> 200 us  [run(): pl.pallas_call(lambda *refs: kernel(ratio, *refs), out_shape=jax.ShapeDty...]
where the time goes in v2:
time: 213 us
  Pallas kernels  200 us (94%)
  local copies, waits for them, and re-layouts  7.16 us (3%)
  other arithmetic  3.75 us (2%)
    pallas_call x1, Pallas kernels, run(): pl.pallas_call(lambda *refs: kernel(ratio, *refs), out_shape=jax.ShapeDty...  200 us

profile of v2, /device:TPU:1, one launch (start us, length us, event | category | flops | bytes accessed | tf_op | source)
XLA Modules:
  0.0 212.5 jit_solution(13357529189896420080)
XLA Ops:
  0.0 1.2 dynamic_slice.28
  3.2 0.7 fusion.6
  3.9 0.7 and_select_fusion.1
  4.6 0.2 convert_reduce_fusion
  4.8 0.8 fusion.5.refs_10_
  5.5 0.0 copy-start
  5.5 0.2 fusion.2
  5.7 0.0 copy-start.1
  5.8 0.6 select_reduce_fusion.refs_9_
  6.3 0.6 select_reduce_fusion.1.refs_7_
  7.0 1.3 dynamic-slice_bitcast_fusion.refs_4_
  8.3 1.6 dynamic_slice.31
  9.8 0.0 copy-done
  9.8 0.0 copy-done.1
  9.8 199.6 %shard_map.82 = bf16[16,128,512]{2,1,0:T(8,128)(2,1)} custom-call(bf16[8,128,2048]{2,1,0:T(8,128)(2,1)} %refs_0_.1, bf16[16,16,2048]{2,1,0:T(8,128)(2,1)} %bitcast.16, bf16[256,2048]{1,0:T(8,128)(2,1)} %bitcast.17, bf16[16,128,512]{2,1,0:T(8,128)(2,1)} %bitcast.18, s32[16,128]{1,0:T(8,128)} %dynamic-slice_bitcast_fusion.refs_4_, s32[16,128]{1,0:T(8,128)} %bitcast.19, ...), custom_call_target="tpu_custom_call" | custom-call | tf_op jit(solution)/shard_map/pallas_call | solution.py:659
  209.5 3.0 %copy.10 = bf16[1,2048,512]{2,1,0:T(8,128)(2,1)} copy(bf16[1,2048,512]{2,1,0:T(8,128)(2,1)} %bitcast.15) | data formatting | bytes 4194304
  (2 shorter events, 0.0 us)
Async XLA Ops:
  5.5 4.3 %copy-start = (s32[16]{0:T(128)}, s32[16]{0:T(128)S(1)}, u32[]{:S(2)}) copy-start(s32[16]{0:T(128)S(1)} %fusion.5.refs_10_) | copy-start | bytes 196
  5.7 4.1 %copy-start.1 = (s32[16]{0:T(128)}, s32[16]{0:T(128)S(1)}, u32[]{:S(2)}) copy-start(s32[16]{0:T(128)S(1)} %multiply_add_fusion.refs_8_) | copy-start | bytes 196

commit v3 on v2

--- a/solution.py
+++ b/solution.py
@@ -223,6 +223,8 @@
 
         lax.fori_loop(0, q_count, make_turned, 0)
         lax.fori_loop(0, g_count - 1, rho_start, 0)
+        if h == 0:
+            own_x.start()
         for i in range(CAP):
             rho_rx[h][ga * CAP + i] = res[h][block_of_slot[ga * CAP + i]]
 
@@ -234,7 +236,6 @@
     next_x.from_plus()
     to_neighbours(2, plus(x), fwd.at[plus(x)])
     next_x.forward()
-    own_x.start()
 
     def make_turn_back(j, carry):
         turn_back[j] = turn_of(j).T.astype(BF16)
@@ -314,20 +315,6 @@
 
     own_x.finish()
     keep.wait()
-    d1_sem, d2_sem = sems(q_count), sems(q_count)
-
-    def spread_copy(d):
-        to = (pb + d) % q_count
-        return copy(dmat.at[to], spread.at[pb], d1_sem + d, (to, ga))
-
-    def spread_start(d, carry):
-        spread_copy(d).start()
-        return carry
-
-    lax.fori_loop(1, q_count, spread_start, 0)
-    keep_d1 = pltpu.make_async_copy(dmat.at[pb], spread.at[pb], local_sem.at[2])
-    keep_d1.start()
-
     for h in parts:
         arrive(part_rx.at[h], part_sem + h)
         project(y, part_rx.at[h], acc2.at[h], True)
@@ -339,36 +326,50 @@
     for k, s in enumerate((x, minus(x), plus(x), beyond(x))):
         arrive(held.at[down, s], y_sem + k)
         arrive(held.at[up, s], y_sem + 4 + k)
-    def spread_wait(d, carry):
-        arrive(spread.at[(pb + q_count - d) % q_count], d1_sem + d)
-        return carry
-
-    lax.fori_loop(1, q_count, spread_wait, 0)
-    keep_d1.wait()
-
-    def choose(q, carry):
-        chosen[q] = spread[minus_q[q]]
-        return carry
-
-    lax.fori_loop(0, q_count, choose, 0)
-
-    def mate_copy(d):
+    d1_sem, d2_sem = sems(q_count), sems(q_count)
+
+    def spread_copy(d):
         to = (pb + d) % q_count
-        return copy(chosen.at[to], mate_rows.at[pb], d2_sem + d, (to, ga))
-
-    def mate_start(d, carry):
-        mate_copy(d).start()
-        return carry
-
-    lax.fori_loop(1, q_count, mate_start, 0)
-    keep_d2 = pltpu.make_async_copy(chosen.at[pb], mate_rows.at[pb], local_sem.at[2])
-    keep_d2.start()
+        return copy(dmat.at[to], spread.at[pb], d1_sem + d, (to, ga))
+
+    def spread_start(d, carry):
+        spread_copy(d).start()
+        return carry
+
+    lax.fori_loop(1, q_count, spread_start, 0)
+    keep_d1 = pltpu.make_async_copy(dmat.at[pb], spread.at[pb], local_sem.at[2])
+    keep_d1.start()
 
     for h in parts:
         for row in (down, up):
             rho_group[...] = group(h, row)
             project(row, rho_group, acc.at[h], False)
         reduce1[h].start()
+    def spread_wait(d, carry):
+        arrive(spread.at[(pb + q_count - d) % q_count], d1_sem + d)
+        return carry
+
+    lax.fori_loop(1, q_count, spread_wait, 0)
+    keep_d1.wait()
+
+    def choose(q, carry):
+        chosen[q] = spread[minus_q[q]]
+        return carry
+
+    lax.fori_loop(0, q_count, choose, 0)
+
+    def mate_copy(d):
+        to = (pb + d) % q_count
+        return copy(chosen.at[to], mate_rows.at[pb], d2_sem + d, (to, ga))
+
+    def mate_start(d, carry):
+        mate_copy(d).start()
+        return carry
+
+    lax.fori_loop(1, q_count, mate_start, 0)
+    keep_d2 = pltpu.make_async_copy(chosen.at[pb], mate_rows.at[pb], local_sem.at[2])
+    keep_d2.start()
+
     for h in parts:
         mate_sum[h, 0] = reduce2[h].finish().astype(BF16)
         send(mate_sum.at[h, 0], mate_sum.at[h, 1], part_sem + 2 + h, on_y(across))

time: 213 us -> 221 us (1.038)
  Pallas kernels: 200 us -> 207 us
    pallas_call x1, Pallas kernels: 200 us -> 207 us  [run(): pl.pallas_call(lambda *refs: kernel(ratio, *refs), out_shape=jax.ShapeDty...]
where the time goes in v3:
time: 221 us; the launch traced here: 220 us
  Pallas kernels  207 us (94%)
  local copies, waits for them, and re-layouts  7.16 us (3%)
  other arithmetic  3.75 us (2%)
    pallas_call x1, Pallas kernels, run(): pl.pallas_call(lambda *refs: kernel(ratio, *refs), out_shape=jax.ShapeDty...  207 us

profile of v3, /device:TPU:1, one launch (start us, length us, event | category | flops | bytes accessed | tf_op | source)
XLA Modules:
  0.0 219.6 jit_solution(9107864467035773427)
XLA Ops:
  0.0 1.2 dynamic_slice.28
  3.2 0.7 fusion.6
  3.9 0.7 and_select_fusion.1
  4.6 0.2 convert_reduce_fusion
  4.8 0.8 fusion.5.refs_10_
  5.5 0.0 copy-start
  5.5 0.2 fusion.2
  5.7 0.0 copy-start.1
  5.8 0.6 select_reduce_fusion.refs_9_
  6.3 0.6 select_reduce_fusion.1.refs_7_
  7.0 1.3 dynamic-slice_bitcast_fusion.refs_4_
  8.3 1.6 dynamic_slice.31
  9.8 0.0 copy-done
  9.8 0.0 copy-done.1
  9.8 206.7 %shard_map.82 = bf16[16,128,512]{2,1,0:T(8,128)(2,1)} custom-call(bf16[8,128,2048]{2,1,0:T(8,128)(2,1)} %refs_0_.1, bf16[16,16,2048]{2,1,0:T(8,128)(2,1)} %bitcast.16, bf16[256,2048]{1,0:T(8,128)(2,1)} %bitcast.17, bf16[16,128,512]{2,1,0:T(8,128)(2,1)} %bitcast.18, s32[16,128]{1,0:T(8,128)} %dynamic-slice_bitcast_fusion.refs_4_, s32[16,128]{1,0:T(8,128)} %bitcast.19, ...), custom_call_target="tpu_custom_call" | custom-call | tf_op jit(solution)/shard_map/pallas_call | solution.py:660
  216.5 3.0 %copy.10 = bf16[1,2048,512]{2,1,0:T(8,128)(2,1)} copy(bf16[1,2048,512]{2,1,0:T(8,128)(2,1)} %bitcast.15) | data formatting | bytes 4194304
  (2 shorter events, 0.0 us)
Async XLA Ops:
  5.5 4.3 %copy-start = (s32[16]{0:T(128)}, s32[16]{0:T(128)S(1)}, u32[]{:S(2)}) copy-start(s32[16]{0:T(128)S(1)} %fusion.5.refs_10_) | copy-start | bytes 196
  5.7 4.1 %copy-start.1 = (s32[16]{0:T(128)}, s32[16]{0:T(128)S(1)}, u32[]{:S(2)}) copy-start(s32[16]{0:T(128)S(1)} %multiply_add_fusion.refs_8_) | copy-start | bytes 196

commit v4 on v2

--- a/solution.py
+++ b/solution.py
@@ -53,7 +53,7 @@
     own_d,
     spread,
     chosen,
-    mate_rows,
+    dcols,
     mate_cols,
     mate_t,
     screened,
@@ -259,7 +259,26 @@
         lax.fori_loop(0, g_count, one, 0)
 
     part_sem = sems(4)
-    for h in parts:
+    column_sem = sems(g_count)
+
+    def column_copy(d):
+        to = (ga + d) % g_count
+        columns = pl.ds(pl.multiple_of(to * basis, basis), basis)
+        return copy(dmat.at[:, :, columns], dcols.at[ga], column_sem + d, (pb, to))
+
+    def column_start(d, carry):
+        column_copy(d).start()
+        return carry
+
+    own_columns = pl.ds(pl.multiple_of(ga * basis, basis), basis)
+    keep_cols = pltpu.make_async_copy(
+        dmat.at[:, :, own_columns], dcols.at[ga], local_sem.at[4]
+    )
+
+    for h in parts:
+        if h:
+            lax.fori_loop(1, g_count, column_start, 0)
+            keep_cols.start()
 
         def rho_wait(d, carry):
             source = (ga + g_count - d) % g_count
@@ -314,18 +333,24 @@
 
     own_x.finish()
     keep.wait()
+    def column_wait(d, carry):
+        arrive(dcols.at[(ga + g_count - d) % g_count], column_sem + d)
+        return carry
+
+    lax.fori_loop(1, g_count, column_wait, 0)
+    keep_cols.wait()
     d1_sem, d2_sem = sems(q_count), sems(q_count)
 
     def spread_copy(d):
         to = (pb + d) % q_count
-        return copy(dmat.at[to], spread.at[pb], d1_sem + d, (to, ga))
+        return copy(dcols.at[to // 2, to % 2], spread.at[pb], d1_sem + d, (to, ga))
 
     def spread_start(d, carry):
         spread_copy(d).start()
         return carry
 
     lax.fori_loop(1, q_count, spread_start, 0)
-    keep_d1 = pltpu.make_async_copy(dmat.at[pb], spread.at[pb], local_sem.at[2])
+    keep_d1 = pltpu.make_async_copy(dcols.at[pb // 2, pb % 2], spread.at[pb], local_sem.at[2])
     keep_d1.start()
 
     for h in parts:
@@ -354,14 +379,14 @@
 
     def mate_copy(d):
         to = (pb + d) % q_count
-        return copy(chosen.at[to], mate_rows.at[pb], d2_sem + d, (to, ga))
+        return copy(chosen.at[to], mate_cols.at[pb], d2_sem + d, (to, ga))
 
     def mate_start(d, carry):
         mate_copy(d).start()
         return carry
 
     lax.fori_loop(1, q_count, mate_start, 0)
-    keep_d2 = pltpu.make_async_copy(chosen.at[pb], mate_rows.at[pb], local_sem.at[2])
+    keep_d2 = pltpu.make_async_copy(chosen.at[pb], mate_cols.at[pb], local_sem.at[2])
     keep_d2.start()
 
     for h in parts:
@@ -373,31 +398,6 @@
         mate_sum[h, 0] = reduce2[h].finish().astype(BF16)
         send(mate_sum.at[h, 0], mate_sum.at[h, 1], part_sem + 2 + h, on_y(across))
         reduce1[h].along_z()
-
-    def mate_wait(d, carry):
-        arrive(mate_rows.at[(pb + q_count - d) % q_count], d2_sem + d)
-        return carry
-
-    lax.fori_loop(1, q_count, mate_wait, 0)
-    keep_d2.wait()
-
-    column_sem = sems(g_count)
-
-    def column_copy(d):
-        to = (ga + d) % g_count
-        columns = pl.ds(pl.multiple_of(to * basis, basis), basis)
-        return copy(mate_rows.at[:, :, columns], mate_cols.at[ga], column_sem + d, (pb, to))
-
-    def column_start(d, carry):
-        column_copy(d).start()
-        return carry
-
-    lax.fori_loop(1, g_count, column_start, 0)
-    own_columns = pl.ds(pl.multiple_of(ga * basis, basis), basis)
-    keep_cols = pltpu.make_async_copy(
-        mate_rows.at[:, :, own_columns], mate_cols.at[ga], local_sem.at[4]
-    )
-    keep_cols.start()
 
     class Gather:
         def __init__(self, ref, use):
@@ -431,10 +431,6 @@
                 arrive(self.ref.at[source], self.i + 4 + d)
                 self.use(source)
 
-    def column_wait(d, carry):
-        arrive(mate_cols.at[(ga + g_count - d) % g_count], column_sem + d)
-        return carry
-
     def apply(h):
         def use(n):
             columns = pl.ds(pl.multiple_of(n * basis, basis), basis)
@@ -450,16 +446,21 @@
         arrive(mate_sum.at[h, 1], part_sem + 2 + h)
         coef[h, ga] = (value + mate_sum[h, 1].astype(F32)).astype(BF16).T
         gather_coef[h].start()
-    lax.fori_loop(1, g_count, column_wait, 0)
-    keep_cols.wait()
+
+    def mate_wait(d, carry):
+        arrive(mate_cols.at[(pb + q_count - d) % q_count], d2_sem + d)
+        return carry
+
+    lax.fori_loop(1, q_count, mate_wait, 0)
+    keep_d2.wait()
     load_d.wait()
-
-    def turn_columns(n, carry):
-        columns = pl.ds(pl.multiple_of(n * basis, basis), basis)
-        mate_t[:, columns] = mate_cols[n].reshape(basis, basis).T
-        return carry
-
-    lax.fori_loop(0, g_count, turn_columns, 0)
+    chunk = mate_cols.shape[1]
+
+    def turn_columns(k, carry):
+        mate_t[:, pl.ds(pl.multiple_of(k * chunk, chunk), chunk)] = mate_cols[k].T
+        return carry
+
+    lax.fori_loop(0, q_count, turn_columns, 0)
     slab_sum[...] = jnp.zeros_like(slab_sum)
 
     half = NX // 2
@@ -650,7 +651,7 @@
     slab = (wide, basis_rows)
     square = (basis_rows, wide)
     slots = (slot_count, block_rows, wide)
-    chunk = basis_rows // q_count
+    chunk = width // q_count
     any_spec = pl.BlockSpec(memory_space=pl.ANY)
     smem_spec = pl.BlockSpec(memory_space=pltpu.SMEM)
     vmem_spec = pl.BlockSpec(memory_space=pltpu.VMEM)
@@ -683,10 +684,10 @@
                 vmem((2, g_count, *square), BF16),
                 vmem((2, *square), F32),
                 vmem((basis_rows, width), BF16),
-                vmem((q_count, chunk, width), BF16),
-                vmem((q_count, chunk, width), BF16),
-                vmem((q_count, chunk, width), BF16),
-                vmem((g_count, q_count, chunk, basis_rows), BF16),
+                vmem((q_count, chunk, basis_rows), BF16),
+                vmem((q_count, chunk, basis_rows), BF16),
+                vmem((g_count, 2, chunk, basis_rows), BF16),
+                vmem((q_count, chunk, basis_rows), BF16),
                 vmem((basis_rows, width), BF16),
                 vmem((2, g_count, *square), BF16),
                 vmem((2, g_count, *square), BF16),
@@ -707,7 +708,7 @@
 
     out = run(
         irr_vectors,
-        inv_dielectric[0].reshape(q_count, chunk, width),
+        inv_dielectric[0].reshape(2, chunk, width),
         inv_dielectric[0],
         pair_density[0].reshape(q_count, block_rows, density_width),
         row_table,

time: 213 us -> 202 us (0.948)
  Pallas kernels: 200 us -> 188 us
    pallas_call x1, Pallas kernels: 200 us -> 188 us  [run(): pl.pallas_call(lambda *refs: kernel(ratio, *refs), out_shape=jax.ShapeDty...]
where the time goes in v4:
time: 202 us; the launch traced here: 201 us
  Pallas kernels  188 us (93%)
  local copies, waits for them, and re-layouts  7.16 us (4%)
  other arithmetic  3.75 us (2%)
    pallas_call x1, Pallas kernels, run(): pl.pallas_call(lambda *refs: kernel(ratio, *refs), out_shape=jax.ShapeDty...  188 us

profile of v4, /device:TPU:1, one launch (start us, length us, event | category | flops | bytes accessed | tf_op | source)
XLA Modules:
  0.0 201.3 jit_solution(3814026989407995856)
XLA Ops:
  0.0 1.2 dynamic_slice.28
  3.2 0.7 fusion.6
  3.9 0.7 and_select_fusion.1
  4.6 0.2 convert_reduce_fusion
  4.8 0.8 fusion.5.refs_10_
  5.5 0.0 copy-start
  5.5 0.2 fusion.2
  5.7 0.0 copy-start.1
  5.8 0.6 select_reduce_fusion.refs_9_
  6.3 0.6 select_reduce_fusion.1.refs_7_
  7.0 1.3 dynamic-slice_bitcast_fusion.refs_4_
  8.3 1.6 dynamic_slice.31
  9.8 0.0 copy-done
  9.8 0.0 copy-done.1
  9.8 188.4 %shard_map.82 = bf16[16,128,512]{2,1,0:T(8,128)(2,1)} custom-call(bf16[8,128,2048]{2,1,0:T(8,128)(2,1)} %refs_0_.1, bf16[2,128,2048]{2,1,0:T(8,128)(2,1)} %bitcast.16, bf16[256,2048]{1,0:T(8,128)(2,1)} %bitcast.17, bf16[16,128,512]{2,1,0:T(8,128)(2,1)} %bitcast.18, s32[16,128]{1,0:T(8,128)} %dynamic-slice_bitcast_fusion.refs_4_, s32[16,128]{1,0:T(8,128)} %bitcast.19, ...), custom_call_target="tpu_custom_call" | custom-call | tf_op jit(solution)/shard_map/pallas_call | solution.py:660
  198.3 3.0 %copy.10 = bf16[1,2048,512]{2,1,0:T(8,128)(2,1)} copy(bf16[1,2048,512]{2,1,0:T(8,128)(2,1)} %bitcast.15) | data formatting | bytes 4194304
  (2 shorter events, 0.0 us)
Async XLA Ops:
  5.5 4.3 %copy-start = (s32[16]{0:T(128)}, s32[16]{0:T(128)S(1)}, u32[]{:S(2)}) copy-start(s32[16]{0:T(128)S(1)} %fusion.5.refs_10_) | copy-start | bytes 196
  5.7 4.1 %copy-start.1 = (s32[16]{0:T(128)}, s32[16]{0:T(128)S(1)}, u32[]{:S(2)}) copy-start(s32[16]{0:T(128)S(1)} %multiply_add_fusion.refs_8_) | copy-start | bytes 196

commit v5 on v4

--- a/solution.py
+++ b/solution.py
@@ -333,26 +333,6 @@
 
     own_x.finish()
     keep.wait()
-    def column_wait(d, carry):
-        arrive(dcols.at[(ga + g_count - d) % g_count], column_sem + d)
-        return carry
-
-    lax.fori_loop(1, g_count, column_wait, 0)
-    keep_cols.wait()
-    d1_sem, d2_sem = sems(q_count), sems(q_count)
-
-    def spread_copy(d):
-        to = (pb + d) % q_count
-        return copy(dcols.at[to // 2, to % 2], spread.at[pb], d1_sem + d, (to, ga))
-
-    def spread_start(d, carry):
-        spread_copy(d).start()
-        return carry
-
-    lax.fori_loop(1, q_count, spread_start, 0)
-    keep_d1 = pltpu.make_async_copy(dcols.at[pb // 2, pb % 2], spread.at[pb], local_sem.at[2])
-    keep_d1.start()
-
     for h in parts:
         arrive(part_rx.at[h], part_sem + h)
         project(y, part_rx.at[h], acc2.at[h], True)
@@ -364,36 +344,56 @@
     for k, s in enumerate((x, minus(x), plus(x), beyond(x))):
         arrive(held.at[down, s], y_sem + k)
         arrive(held.at[up, s], y_sem + 4 + k)
-    def spread_wait(d, carry):
-        arrive(spread.at[(pb + q_count - d) % q_count], d1_sem + d)
-        return carry
-
-    lax.fori_loop(1, q_count, spread_wait, 0)
-    keep_d1.wait()
-
-    def choose(q, carry):
-        chosen[q] = spread[minus_q[q]]
-        return carry
-
-    lax.fori_loop(0, q_count, choose, 0)
-
-    def mate_copy(d):
+    def column_wait(d, carry):
+        arrive(dcols.at[(ga + g_count - d) % g_count], column_sem + d)
+        return carry
+
+    lax.fori_loop(1, g_count, column_wait, 0)
+    keep_cols.wait()
+    d1_sem, d2_sem = sems(q_count), sems(q_count)
+
+    def spread_copy(d):
         to = (pb + d) % q_count
-        return copy(chosen.at[to], mate_cols.at[pb], d2_sem + d, (to, ga))
-
-    def mate_start(d, carry):
-        mate_copy(d).start()
-        return carry
-
-    lax.fori_loop(1, q_count, mate_start, 0)
-    keep_d2 = pltpu.make_async_copy(chosen.at[pb], mate_cols.at[pb], local_sem.at[2])
-    keep_d2.start()
+        return copy(dcols.at[to // 2, to % 2], spread.at[pb], d1_sem + d, (to, ga))
+
+    def spread_start(d, carry):
+        spread_copy(d).start()
+        return carry
+
+    lax.fori_loop(1, q_count, spread_start, 0)
+    keep_d1 = pltpu.make_async_copy(dcols.at[pb // 2, pb % 2], spread.at[pb], local_sem.at[2])
+    keep_d1.start()
 
     for h in parts:
         for row in (down, up):
             rho_group[...] = group(h, row)
             project(row, rho_group, acc.at[h], False)
         reduce1[h].start()
+    def spread_wait(d, carry):
+        arrive(spread.at[(pb + q_count - d) % q_count], d1_sem + d)
+        return carry
+
+    lax.fori_loop(1, q_count, spread_wait, 0)
+    keep_d1.wait()
+
+    def choose(q, carry):
+        chosen[q] = spread[minus_q[q]]
+        return carry
+
+    lax.fori_loop(0, q_count, choose, 0)
+
+    def mate_copy(d):
+        to = (pb + d) % q_count
+        return copy(chosen.at[to], mate_cols.at[pb], d2_sem + d, (to, ga))
+
+    def mate_start(d, carry):
+        mate_copy(d).start()
+        return carry
+
+    lax.fori_loop(1, q_count, mate_start, 0)
+    keep_d2 = pltpu.make_async_copy(chosen.at[pb], mate_cols.at[pb], local_sem.at[2])
+    keep_d2.start()
+
     for h in parts:
         mate_sum[h, 0] = reduce2[h].finish().astype(BF16)
         send(mate_sum.at[h, 0], mate_sum.at[h, 1], part_sem + 2 + h, on_y(across))

time: 202 us -> 201 us (level)
  no operation moved by 1% of the time
where the time goes in v5:
time: 201 us
  Pallas kernels  188 us (94%)
  local copies, waits for them, and re-layouts  7.16 us (4%)
  other arithmetic  3.75 us (2%)
    pallas_call x1, Pallas kernels, run(): pl.pallas_call(lambda *refs: kernel(ratio, *refs), out_shape=jax.ShapeDty...  188 us

profile of v5, /device:TPU:1, one launch (start us, length us, event | category | flops | bytes accessed | tf_op | source)
XLA Modules:
  0.0 200.6 jit_solution(16455112962528149339)
XLA Ops:
  0.0 1.2 dynamic_slice.28
  3.2 0.7 fusion.6
  3.9 0.7 and_select_fusion.1
  4.6 0.2 convert_reduce_fusion
  4.8 0.8 fusion.5.refs_10_
  5.5 0.0 copy-start
  5.5 0.2 fusion.2
  5.7 0.0 copy-start.1
  5.8 0.6 select_reduce_fusion.refs_9_
  6.3 0.6 select_reduce_fusion.1.refs_7_
  7.0 1.3 dynamic-slice_bitcast_fusion.refs_4_
  8.3 1.6 dynamic_slice.31
  9.8 0.0 copy-done
  9.8 0.0 copy-done.1
  9.8 187.7 %shard_map.82 = bf16[16,128,512]{2,1,0:T(8,128)(2,1)} custom-call(bf16[8,128,2048]{2,1,0:T(8,128)(2,1)} %refs_0_.1, bf16[2,128,2048]{2,1,0:T(8,128)(2,1)} %bitcast.16, bf16[256,2048]{1,0:T(8,128)(2,1)} %bitcast.17, bf16[16,128,512]{2,1,0:T(8,128)(2,1)} %bitcast.18, s32[16,128]{1,0:T(8,128)} %dynamic-slice_bitcast_fusion.refs_4_, s32[16,128]{1,0:T(8,128)} %bitcast.19, ...), custom_call_target="tpu_custom_call" | custom-call | tf_op jit(solution)/shard_map/pallas_call | solution.py:660
  197.5 3.0 %copy.10 = bf16[1,2048,512]{2,1,0:T(8,128)(2,1)} copy(bf16[1,2048,512]{2,1,0:T(8,128)(2,1)} %bitcast.15) | data formatting | bytes 4194304
  (2 shorter events, 0.0 us)
Async XLA Ops:
  5.5 4.3 %copy-start = (s32[16]{0:T(128)}, s32[16]{0:T(128)S(1)}, u32[]{:S(2)}) copy-start(s32[16]{0:T(128)S(1)} %fusion.5.refs_10_) | copy-start | bytes 196
  5.7 4.1 %copy-start.1 = (s32[16]{0:T(128)}, s32[16]{0:T(128)S(1)}, u32[]{:S(2)}) copy-start(s32[16]{0:T(128)S(1)} %multiply_add_fusion.refs_8_) | copy-start | bytes 196

commit v6 on v5

--- a/solution.py
+++ b/solution.py
@@ -502,14 +502,14 @@
         gather_coef[h].rest()
         screened[h, ga] = (0.5 * slab_sum[h] - coef[h, ga].astype(F32)).astype(BF16)
         send(screened.at[h, ga], mate_scr.at[h, ga], mate_sem + h, on_y(across))
-        gather_own[h].start()
+        if h == 0:
+            gather_own[h].start()
     for h in parts:
         reduce1[h].sent()
         reduce2[h].sent()
-    for h in parts:
-        gather_own[h].own()
-        arrive(mate_scr.at[h, ga], mate_sem + h)
-        gather_mate[h].start()
+    gather_own[0].own()
+    arrive(mate_scr.at[0, ga], mate_sem)
+    gather_mate[0].start()
 
     def rho_sent(d, carry):
         for h in parts:
@@ -529,11 +529,17 @@
         )
 
     for h in parts:
+        if h:
+            gather_own[h].own()
         gather_own[h].beside()
         gather_own[h].along_z()
         gather_mate[h].own()
         gather_mate[h].beside()
         gather_mate[h].along_z()
+        if h == 0:
+            gather_own[1].start()
+            arrive(mate_scr.at[1, ga], mate_sem + 1)
+            gather_mate[1].start()
         gather_mate[h].rest()
         mate_res[h] = (acc[h, :half] * ratio).astype(BF16).reshape(NX, rows, wide)
         send(mate_res.at[h], res[h].at[pl.ds(y * NX, NX)], mate_sem + 2 + h, on_y(across))

time: 201 us -> 198 us (0.985)
  Pallas kernels: 188 us -> 185 us
    pallas_call x1, Pallas kernels: 188 us -> 185 us  [run(): pl.pallas_call(lambda *refs: kernel(ratio, *refs), out_shape=jax.ShapeDty...]
where the time goes in v6:
time: 198 us
  Pallas kernels  185 us (93%)
  local copies, waits for them, and re-layouts  7.16 us (4%)
  other arithmetic  3.75 us (2%)
    pallas_call x1, Pallas kernels, run(): pl.pallas_call(lambda *refs: kernel(ratio, *refs), out_shape=jax.ShapeDty...  185 us

profile of v6, /device:TPU:1, one launch (start us, length us, event | category | flops | bytes accessed | tf_op | source)
XLA Modules:
  0.0 197.9 jit_solution(1328296995512063771)
XLA Ops:
  0.0 1.2 dynamic_slice.28
  3.2 0.7 fusion.6
  3.9 0.7 and_select_fusion.1
  4.6 0.2 convert_reduce_fusion
  4.8 0.8 fusion.5.refs_10_
  5.5 0.0 copy-start
  5.5 0.2 fusion.2
  5.7 0.0 copy-start.1
  5.8 0.6 select_reduce_fusion.refs_9_
  6.3 0.6 select_reduce_fusion.1.refs_7_
  7.0 1.3 dynamic-slice_bitcast_fusion.refs_4_
  8.3 1.6 dynamic_slice.31
  9.8 0.0 copy-done
  9.8 0.0 copy-done.1
  9.8 185.0 %shard_map.82 = bf16[16,128,512]{2,1,0:T(8,128)(2,1)} custom-call(bf16[8,128,2048]{2,1,0:T(8,128)(2,1)} %refs_0_.1, bf16[2,128,2048]{2,1,0:T(8,128)(2,1)} %bitcast.16, bf16[256,2048]{1,0:T(8,128)(2,1)} %bitcast.17, bf16[16,128,512]{2,1,0:T(8,128)(2,1)} %bitcast.18, s32[16,128]{1,0:T(8,128)} %dynamic-slice_bitcast_fusion.refs_4_, s32[16,128]{1,0:T(8,128)} %bitcast.19, ...), custom_call_target="tpu_custom_call" | custom-call | tf_op jit(solution)/shard_map/pallas_call | solution.py:666
  194.9 3.0 %copy.10 = bf16[1,2048,512]{2,1,0:T(8,128)(2,1)} copy(bf16[1,2048,512]{2,1,0:T(8,128)(2,1)} %bitcast.15) | data formatting | bytes 4194304
  (2 shorter events, 0.0 us)
Async XLA Ops:
  5.5 4.3 %copy-start = (s32[16]{0:T(128)}, s32[16]{0:T(128)S(1)}, u32[]{:S(2)}) copy-start(s32[16]{0:T(128)S(1)} %fusion.5.refs_10_) | copy-start | bytes 196
  5.7 4.1 %copy-start.1 = (s32[16]{0:T(128)}, s32[16]{0:T(128)S(1)}, u32[]{:S(2)}) copy-start(s32[16]{0:T(128)S(1)} %multiply_add_fusion.refs_8_) | copy-start | bytes 196

commit v7 on v6

--- a/solution.py
+++ b/solution.py
@@ -245,13 +245,17 @@
     to_neighbours(3, beyond(x), fwd.at[beyond(x)])
     own_x.forward()
 
-    def group(h, row):
-        return jnp.concatenate([rho_rx[h][held_slot[row * NX + i]] for i in range(NX)], axis=0).T
-
-    def project(row, values, total, first):
+    def row_blocks(row):
+        return [(row, i) for i in range(NX)]
+
+    def group(h, blocks):
+        found = [rho_rx[h][held_slot[row * NX + i]] for row, i in blocks]
+        return jnp.concatenate(found, axis=0).T
+
+    def project(blocks, values, total, first):
         def one(n, carry):
             columns = pl.ds(pl.multiple_of(n * basis, basis), basis)
-            block = held[row, :, :, columns].reshape(-1, basis)
+            block = jnp.concatenate([held[row, i, :, columns] for row, i in blocks], axis=0)
             part = jnp.dot(values[...], block, preferred_element_type=F32)
             total[n] = part if first else total[n] + part
             return carry
@@ -286,7 +290,7 @@
             return carry
 
         lax.fori_loop(1, g_count, rho_wait, 0)
-        part_tx[h] = group(h, across)
+        part_tx[h] = group(h, row_blocks(across))
         send(part_tx.at[h], part_rx.at[h], part_sem + h, on_y(across))
 
     class Reduce:
@@ -335,15 +339,25 @@
     keep.wait()
     for h in parts:
         arrive(part_rx.at[h], part_sem + h)
-        project(y, part_rx.at[h], acc2.at[h], True)
+        project(row_blocks(y), part_rx.at[h], acc2.at[h], True)
         reduce2[h].start()
     for h in parts:
-        rho_group[...] = group(h, y)
-        project(y, rho_group, acc.at[h], True)
+        rho_group[...] = group(h, row_blocks(y))
+        project(row_blocks(y), rho_group, acc.at[h], True)
         reduce2[h].along_z()
-    for k, s in enumerate((x, minus(x), plus(x), beyond(x))):
-        arrive(held.at[down, s], y_sem + k)
-        arrive(held.at[up, s], y_sem + 4 + k)
+    order = (x, minus(x), plus(x), beyond(x))
+    batches = [[(row, s) for s in order[k : k + 2] for row in (down, up)] for k in (0, 2)]
+
+    def batch_in(first):
+        for k in (first, first + 1):
+            arrive(held.at[down, order[k]], y_sem + k)
+            arrive(held.at[up, order[k]], y_sem + 4 + k)
+
+    batch_in(0)
+    for h in parts:
+        rho_group[...] = group(h, batches[0])
+        project(batches[0], rho_group, acc.at[h], False)
+    batch_in(2)
     def column_wait(d, carry):
         arrive(dcols.at[(ga + g_count - d) % g_count], column_sem + d)
         return carry
@@ -365,9 +379,8 @@
     keep_d1.start()
 
     for h in parts:
-        for row in (down, up):
-            rho_group[...] = group(h, row)
-            project(row, rho_group, acc.at[h], False)
+        rho_group[...] = group(h, batches[1])
+        project(batches[1], rho_group, acc.at[h], False)
         reduce1[h].start()
     def spread_wait(d, carry):
         arrive(spread.at[(pb + q_count - d) % q_count], d1_sem + d)

time: 198 us -> 202 us (1.020)
  Pallas kernels: 185 us -> 189 us
    pallas_call x1, Pallas kernels: 185 us -> 189 us  [run(): pl.pallas_call(lambda *refs: kernel(ratio, *refs), out_shape=jax.ShapeDty...]
where the time goes in v7:
time: 202 us
  Pallas kernels  189 us (94%)
  local copies, waits for them, and re-layouts  7.16 us (4%)
  other arithmetic  3.75 us (2%)
    pallas_call x1, Pallas kernels, run(): pl.pallas_call(lambda *refs: kernel(ratio, *refs), out_shape=jax.ShapeDty...  189 us

profile of v7, /device:TPU:1, one launch (start us, length us, event | category | flops | bytes accessed | tf_op | source)
XLA Modules:
  0.0 201.9 jit_solution(8314737087621739108)
XLA Ops:
  0.0 1.2 dynamic_slice.28
  3.2 0.7 fusion.6
  3.9 0.7 and_select_fusion.1
  4.6 0.2 convert_reduce_fusion
  4.8 0.8 fusion.5.refs_10_
  5.5 0.0 copy-start
  5.5 0.2 fusion.2
  5.7 0.0 copy-start.1
  5.8 0.6 select_reduce_fusion.refs_9_
  6.3 0.6 select_reduce_fusion.1.refs_7_
  7.0 1.3 dynamic-slice_bitcast_fusion.refs_4_
  8.3 1.6 dynamic_slice.31
  9.8 0.0 copy-done
  9.8 0.0 copy-done.1
  9.8 189.0 %shard_map.82 = bf16[16,128,512]{2,1,0:T(8,128)(2,1)} custom-call(bf16[8,128,2048]{2,1,0:T(8,128)(2,1)} %refs_0_.1, bf16[2,128,2048]{2,1,0:T(8,128)(2,1)} %bitcast.16, bf16[256,2048]{1,0:T(8,128)(2,1)} %bitcast.17, bf16[16,128,512]{2,1,0:T(8,128)(2,1)} %bitcast.18, s32[16,128]{1,0:T(8,128)} %dynamic-slice_bitcast_fusion.refs_4_, s32[16,128]{1,0:T(8,128)} %bitcast.19, ...), custom_call_target="tpu_custom_call" | custom-call | tf_op jit(solution)/shard_map/pallas_call | solution.py:679
  198.8 3.0 %copy.10 = bf16[1,2048,512]{2,1,0:T(8,128)(2,1)} copy(bf16[1,2048,512]{2,1,0:T(8,128)(2,1)} %bitcast.15) | data formatting | bytes 4194304
  (2 shorter events, 0.0 us)
Async XLA Ops:
  5.5 4.3 %copy-start = (s32[16]{0:T(128)}, s32[16]{0:T(128)S(1)}, u32[]{:S(2)}) copy-start(s32[16]{0:T(128)S(1)} %fusion.5.refs_10_) | copy-start | bytes 196
  5.7 4.1 %copy-start.1 = (s32[16]{0:T(128)}, s32[16]{0:T(128)S(1)}, u32[]{:S(2)}) copy-start(s32[16]{0:T(128)S(1)} %multiply_add_fusion.refs_8_) | copy-start | bytes 196

commit v8 on v6

--- a/solution.py
+++ b/solution.py
@@ -333,42 +333,43 @@
 
     own_x.finish()
     keep.wait()
-    for h in parts:
+    def column_wait(d, carry):
+        arrive(dcols.at[(ga + g_count - d) % g_count], column_sem + d)
+        return carry
+
+    lax.fori_loop(1, g_count, column_wait, 0)
+    keep_cols.wait()
+    d1_sem, d2_sem = sems(q_count), sems(q_count)
+
+    def spread_copy(d):
+        to = (pb + d) % q_count
+        return copy(dcols.at[to // 2, to % 2], spread.at[pb], d1_sem + d, (to, ga))
+
+    def spread_start(d, carry):
+        spread_copy(d).start()
+        return carry
+
+    lax.fori_loop(1, q_count, spread_start, 0)
+    keep_d1 = pltpu.make_async_copy(dcols.at[pb // 2, pb % 2], spread.at[pb], local_sem.at[2])
+    keep_d1.start()
+
+    for h in parts:
+        rho_group[...] = group(h, y)
+        project(y, rho_group, acc.at[h], True)
         arrive(part_rx.at[h], part_sem + h)
         project(y, part_rx.at[h], acc2.at[h], True)
         reduce2[h].start()
-    for h in parts:
-        rho_group[...] = group(h, y)
-        project(y, rho_group, acc.at[h], True)
-        reduce2[h].along_z()
+    reduce2[0].along_z()
     for k, s in enumerate((x, minus(x), plus(x), beyond(x))):
         arrive(held.at[down, s], y_sem + k)
         arrive(held.at[up, s], y_sem + 4 + k)
-    def column_wait(d, carry):
-        arrive(dcols.at[(ga + g_count - d) % g_count], column_sem + d)
-        return carry
-
-    lax.fori_loop(1, g_count, column_wait, 0)
-    keep_cols.wait()
-    d1_sem, d2_sem = sems(q_count), sems(q_count)
-
-    def spread_copy(d):
-        to = (pb + d) % q_count
-        return copy(dcols.at[to // 2, to % 2], spread.at[pb], d1_sem + d, (to, ga))
-
-    def spread_start(d, carry):
-        spread_copy(d).start()
-        return carry
-
-    lax.fori_loop(1, q_count, spread_start, 0)
-    keep_d1 = pltpu.make_async_copy(dcols.at[pb // 2, pb % 2], spread.at[pb], local_sem.at[2])
-    keep_d1.start()
-
     for h in parts:
         for row in (down, up):
             rho_group[...] = group(h, row)
             project(row, rho_group, acc.at[h], False)
         reduce1[h].start()
+        if h == 0:
+            reduce2[1].along_z()
     def spread_wait(d, carry):
         arrive(spread.at[(pb + q_count - d) % q_count], d1_sem + d)
         return carry

time: 198 us -> 197 us (level)
  no operation moved by 1% of the time
where the time goes in v8:
time: 197 us; the launch traced here: 196 us
  Pallas kernels  184 us (93%)
  local copies, waits for them, and re-layouts  7.16 us (4%)
  other arithmetic  3.75 us (2%)
  between operations  1.97 us (1%)
    pallas_call x1, Pallas kernels, run(): pl.pallas_call(lambda *refs: kernel(ratio, *refs), out_shape=jax.ShapeDty...  184 us

profile of v8, /device:TPU:1, one launch (start us, length us, event | category | flops | bytes accessed | tf_op | source)
XLA Modules:
  0.0 196.5 jit_solution(2996868620220450323)
XLA Ops:
  0.0 1.2 dynamic_slice.28
  3.2 0.7 fusion.6
  3.9 0.7 and_select_fusion.1
  4.6 0.2 convert_reduce_fusion
  4.8 0.8 fusion.5.refs_10_
  5.5 0.0 copy-start
  5.5 0.2 fusion.2
  5.7 0.0 copy-start.1
  5.8 0.6 select_reduce_fusion.refs_9_
  6.3 0.6 select_reduce_fusion.1.refs_7_
  7.0 1.3 dynamic-slice_bitcast_fusion.refs_4_
  8.3 1.6 dynamic_slice.31
  9.8 0.0 copy-done
  9.8 0.0 copy-done.1
  9.8 183.6 %shard_map.82 = bf16[16,128,512]{2,1,0:T(8,128)(2,1)} custom-call(bf16[8,128,2048]{2,1,0:T(8,128)(2,1)} %refs_0_.1, bf16[2,128,2048]{2,1,0:T(8,128)(2,1)} %bitcast.16, bf16[256,2048]{1,0:T(8,128)(2,1)} %bitcast.17, bf16[16,128,512]{2,1,0:T(8,128)(2,1)} %bitcast.18, s32[16,128]{1,0:T(8,128)} %dynamic-slice_bitcast_fusion.refs_4_, s32[16,128]{1,0:T(8,128)} %bitcast.19, ...), custom_call_target="tpu_custom_call" | custom-call | tf_op jit(solution)/shard_map/pallas_call | solution.py:667
  193.4 3.0 %copy.10 = bf16[1,2048,512]{2,1,0:T(8,128)(2,1)} copy(bf16[1,2048,512]{2,1,0:T(8,128)(2,1)} %bitcast.15) | data formatting | bytes 4194304
  (2 shorter events, 0.0 us)
Async XLA Ops:
  5.5 4.3 %copy-start = (s32[16]{0:T(128)}, s32[16]{0:T(128)S(1)}, u32[]{:S(2)}) copy-start(s32[16]{0:T(128)S(1)} %fusion.5.refs_10_) | copy-start | bytes 196
  5.7 4.1 %copy-start.1 = (s32[16]{0:T(128)}, s32[16]{0:T(128)S(1)}, u32[]{:S(2)}) copy-start(s32[16]{0:T(128)S(1)} %multiply_add_fusion.refs_8_) | copy-start | bytes 196

commit v9 on v8

--- a/solution.py
+++ b/solution.py
@@ -276,9 +276,6 @@
     )
 
     for h in parts:
-        if h:
-            lax.fori_loop(1, g_count, column_start, 0)
-            keep_cols.start()
 
         def rho_wait(d, carry):
             source = (ga + g_count - d) % g_count
@@ -288,6 +285,9 @@
         lax.fori_loop(1, g_count, rho_wait, 0)
         part_tx[h] = group(h, across)
         send(part_tx.at[h], part_rx.at[h], part_sem + h, on_y(across))
+
+    lax.fori_loop(1, g_count, column_start, 0)
+    keep_cols.start()
 
     class Reduce:
         def __init__(self, total, landing, outgoing, incoming):
@@ -333,32 +333,32 @@
 
     own_x.finish()
     keep.wait()
-    def column_wait(d, carry):
-        arrive(dcols.at[(ga + g_count - d) % g_count], column_sem + d)
-        return carry
-
-    lax.fori_loop(1, g_count, column_wait, 0)
-    keep_cols.wait()
-    d1_sem, d2_sem = sems(q_count), sems(q_count)
-
-    def spread_copy(d):
-        to = (pb + d) % q_count
-        return copy(dcols.at[to // 2, to % 2], spread.at[pb], d1_sem + d, (to, ga))
-
-    def spread_start(d, carry):
-        spread_copy(d).start()
-        return carry
-
-    lax.fori_loop(1, q_count, spread_start, 0)
-    keep_d1 = pltpu.make_async_copy(dcols.at[pb // 2, pb % 2], spread.at[pb], local_sem.at[2])
-    keep_d1.start()
-
     for h in parts:
         rho_group[...] = group(h, y)
         project(y, rho_group, acc.at[h], True)
         arrive(part_rx.at[h], part_sem + h)
         project(y, part_rx.at[h], acc2.at[h], True)
         reduce2[h].start()
+    def column_wait(d, carry):
+        arrive(dcols.at[(ga + g_count - d) % g_count], column_sem + d)
+        return carry
+
+    lax.fori_loop(1, g_count, column_wait, 0)
+    keep_cols.wait()
+    d1_sem, d2_sem = sems(q_count), sems(q_count)
+
+    def spread_copy(d):
+        to = (pb + d) % q_count
+        return copy(dcols.at[to // 2, to % 2], spread.at[pb], d1_sem + d, (to, ga))
+
+    def spread_start(d, carry):
+        spread_copy(d).start()
+        return carry
+
+    lax.fori_loop(1, q_count, spread_start, 0)
+    keep_d1 = pltpu.make_async_copy(dcols.at[pb // 2, pb % 2], spread.at[pb], local_sem.at[2])
+    keep_d1.start()
+
     reduce2[0].along_z()
     for k, s in enumerate((x, minus(x), plus(x), beyond(x))):
         arrive(held.at[down, s], y_sem + k)

time: 197 us -> 194 us (0.985)
  Pallas kernels: 184 us -> 181 us
    pallas_call x1, Pallas kernels: 184 us -> 181 us  [run(): pl.pallas_call(lambda *refs: kernel(ratio, *refs), out_shape=jax.ShapeDty...]
where the time goes in v9:
time: 194 us; the launch traced here: 193 us
  Pallas kernels  181 us (93%)
  local copies, waits for them, and re-layouts  7.16 us (4%)
  other arithmetic  3.75 us (2%)
  between operations  1.97 us (1%)
    pallas_call x1, Pallas kernels, run(): pl.pallas_call(lambda *refs: kernel(ratio, *refs), out_shape=jax.ShapeDty...  181 us

profile of v9, /device:TPU:1, one launch (start us, length us, event | category | flops | bytes accessed | tf_op | source)
XLA Modules:
  0.0 193.5 jit_solution(13686538506824685548)
XLA Ops:
  0.0 1.2 dynamic_slice.28
  3.2 0.7 fusion.6
  3.9 0.7 and_select_fusion.1
  4.6 0.2 convert_reduce_fusion
  4.8 0.8 fusion.5.refs_10_
  5.5 0.0 copy-start
  5.5 0.2 fusion.2
  5.7 0.0 copy-start.1
  5.8 0.6 select_reduce_fusion.refs_9_
  6.3 0.6 select_reduce_fusion.1.refs_7_
  7.0 1.3 dynamic-slice_bitcast_fusion.refs_4_
  8.3 1.6 dynamic_slice.31
  9.8 0.0 copy-done
  9.8 0.0 copy-done.1
  9.8 180.6 %shard_map.82 = bf16[16,128,512]{2,1,0:T(8,128)(2,1)} custom-call(bf16[8,128,2048]{2,1,0:T(8,128)(2,1)} %refs_0_.1, bf16[2,128,2048]{2,1,0:T(8,128)(2,1)} %bitcast.16, bf16[256,2048]{1,0:T(8,128)(2,1)} %bitcast.17, bf16[16,128,512]{2,1,0:T(8,128)(2,1)} %bitcast.18, s32[16,128]{1,0:T(8,128)} %dynamic-slice_bitcast_fusion.refs_4_, s32[16,128]{1,0:T(8,128)} %bitcast.19, ...), custom_call_target="tpu_custom_call" | custom-call | tf_op jit(solution)/shard_map/pallas_call | solution.py:667
  190.4 3.0 %copy.10 = bf16[1,2048,512]{2,1,0:T(8,128)(2,1)} copy(bf16[1,2048,512]{2,1,0:T(8,128)(2,1)} %bitcast.15) | data formatting | bytes 4194304
  (2 shorter events, 0.0 us)
Async XLA Ops:
  5.5 4.3 %copy-start = (s32[16]{0:T(128)}, s32[16]{0:T(128)S(1)}, u32[]{:S(2)}) copy-start(s32[16]{0:T(128)S(1)} %fusion.5.refs_10_) | copy-start | bytes 196
  5.7 4.1 %copy-start.1 = (s32[16]{0:T(128)}, s32[16]{0:T(128)S(1)}, u32[]{:S(2)}) copy-start(s32[16]{0:T(128)S(1)} %multiply_add_fusion.refs_8_) | copy-start | bytes 196

commit v10 on v9

--- a/solution.py
+++ b/solution.py
@@ -167,6 +167,26 @@
 
     lax.fori_loop(1, q_count, greet_pb, 0)
     lax.fori_loop(1, g_count, greet_ga, 0)
+
+    def turn_of(j):
+        sources = lax.broadcasted_iota(jnp.int32, (rows, rows), 0)
+        sign = (1 - 2 * bits[pl.ds(j, 1), :]).astype(F32)
+        return jnp.where(row_table[pl.ds(j, 1), :] == sources, sign, 0.0)
+
+    def make_turned(h):
+        def one(j, carry):
+            value = jnp.dot(
+                turn_of(j).astype(BF16),
+                out[j, :, h * wide : (h + 1) * wide],
+                preferred_element_type=F32,
+            )
+            res[h][j] = value.astype(BF16)
+            return carry
+
+        lax.fori_loop(0, q_count, one, 0)
+
+    load_rho.wait()
+    make_turned(0)
     pl.semaphore_wait(barrier, q_count + g_count - 2)
 
     own_irr = NX * (y % 2)
@@ -185,12 +205,6 @@
 
     to_neighbours(0, x, irr.at[next_irr + x])
 
-    def turn_of(j):
-        sources = lax.broadcasted_iota(jnp.int32, (rows, rows), 0)
-        sign = (1 - 2 * bits[pl.ds(j, 1), :]).astype(F32)
-        return jnp.where(row_table[pl.ds(j, 1), :] == sources, sign, 0.0)
-
-    load_rho.wait()
     rho_sem = sems(2 * g_count)
 
     def rho_copy(h, d):
@@ -204,15 +218,6 @@
 
     for h in parts:
 
-        def make_turned(j, carry):
-            value = jnp.dot(
-                turn_of(j).astype(BF16),
-                out[j, :, h * wide : (h + 1) * wide],
-                preferred_element_type=F32,
-            )
-            res[h][j] = value.astype(BF16)
-            return carry
-
         def rho_start(k, carry):
             d = (k + 2) % (g_count - 1) + 1
             to = (ga + d) % g_count
@@ -221,7 +226,8 @@
             rho_copy(h, d).start()
             return carry
 
-        lax.fori_loop(0, q_count, make_turned, 0)
+        if h:
+            make_turned(h)
         lax.fori_loop(0, g_count - 1, rho_start, 0)
         for i in range(CAP):
             rho_rx[h][ga * CAP + i] = res[h][block_of_slot[ga * CAP + i]]
@@ -530,10 +536,6 @@
         )
 
     for h in parts:
-        if h:
-            gather_own[h].own()
-        gather_own[h].beside()
-        gather_own[h].along_z()
         gather_mate[h].own()
         gather_mate[h].beside()
         gather_mate[h].along_z()
@@ -544,6 +546,10 @@
         gather_mate[h].rest()
         mate_res[h] = (acc[h, :half] * ratio).astype(BF16).reshape(NX, rows, wide)
         send(mate_res.at[h], res[h].at[pl.ds(y * NX, NX)], mate_sem + 2 + h, on_y(across))
+        if h:
+            gather_own[h].own()
+        gather_own[h].beside()
+        gather_own[h].along_z()
         gather_own[h].rest()
 
         def finish_rows(k, carry):

time: 194 us -> 195 us (level)
  no operation moved by 1% of the time
where the time goes in v10:
time: 195 us; the launch traced here: 194 us
  Pallas kernels  181 us (93%)
  local copies, waits for them, and re-layouts  7.16 us (4%)
  other arithmetic  3.75 us (2%)
  between operations  1.97 us (1%)
    pallas_call x1, Pallas kernels, run(): pl.pallas_call(lambda *refs: kernel(ratio, *refs), out_shape=jax.ShapeDty...  181 us

profile of v10, /device:TPU:1, one launch (start us, length us, event | category | flops | bytes accessed | tf_op | source)
XLA Modules:
  0.0 194.2 jit_solution(4223509759428433068)
XLA Ops:
  0.0 1.2 dynamic_slice.28
  3.2 0.7 fusion.6
  3.9 0.7 and_select_fusion.1
  4.6 0.2 convert_reduce_fusion
  4.8 0.8 fusion.5.refs_10_
  5.5 0.0 copy-start
  5.5 0.2 fusion.2
  5.7 0.0 copy-start.1
  5.8 0.6 select_reduce_fusion.refs_9_
  6.3 0.6 select_reduce_fusion.1.refs_7_
  7.0 1.3 dynamic-slice_bitcast_fusion.refs_4_
  8.3 1.6 dynamic_slice.31
  9.8 0.0 copy-done
  9.8 0.0 copy-done.1
  9.8 181.3 %shard_map.82 = bf16[16,128,512]{2,1,0:T(8,128)(2,1)} custom-call(bf16[8,128,2048]{2,1,0:T(8,128)(2,1)} %refs_0_.1, bf16[2,128,2048]{2,1,0:T(8,128)(2,1)} %bitcast.16, bf16[256,2048]{1,0:T(8,128)(2,1)} %bitcast.17, bf16[16,128,512]{2,1,0:T(8,128)(2,1)} %bitcast.18, s32[16,128]{1,0:T(8,128)} %dynamic-slice_bitcast_fusion.refs_4_, s32[16,128]{1,0:T(8,128)} %bitcast.19, ...), custom_call_target="tpu_custom_call" | custom-call | tf_op jit(solution)/shard_map/pallas_call | solution.py:673
  191.2 3.0 %copy.10 = bf16[1,2048,512]{2,1,0:T(8,128)(2,1)} copy(bf16[1,2048,512]{2,1,0:T(8,128)(2,1)} %bitcast.15) | data formatting | bytes 4194304
  (2 shorter events, 0.0 us)
Async XLA Ops:
  5.5 4.3 %copy-start = (s32[16]{0:T(128)}, s32[16]{0:T(128)S(1)}, u32[]{:S(2)}) copy-start(s32[16]{0:T(128)S(1)} %fusion.5.refs_10_) | copy-start | bytes 196
  5.7 4.1 %copy-start.1 = (s32[16]{0:T(128)}, s32[16]{0:T(128)S(1)}, u32[]{:S(2)}) copy-start(s32[16]{0:T(128)S(1)} %multiply_add_fusion.refs_8_) | copy-start | bytes 196

commit v11 on v9

--- a/solution.py
+++ b/solution.py
@@ -229,12 +229,12 @@
     load_d = pltpu.make_async_copy(drows, own_d, local_sem.at[3])
     load_d.start()
 
+    own_x.start()
     next_x.from_minus()
     to_neighbours(1, minus(x), fwd.at[minus(x)])
     next_x.from_plus()
     to_neighbours(2, plus(x), fwd.at[plus(x)])
     next_x.forward()
-    own_x.start()
 
     def make_turn_back(j, carry):
         turn_back[j] = turn_of(j).T.astype(BF16)

time: 194 us -> 202 us (1.041)
  Pallas kernels: 181 us -> 189 us
    pallas_call x1, Pallas kernels: 181 us -> 189 us  [run(): pl.pallas_call(lambda *refs: kernel(ratio, *refs), out_shape=jax.ShapeDty...]
where the time goes in v11:
time: 202 us
  Pallas kernels  189 us (94%)
  local copies, waits for them, and re-layouts  7.16 us (4%)
  other arithmetic  3.75 us (2%)
    pallas_call x1, Pallas kernels, run(): pl.pallas_call(lambda *refs: kernel(ratio, *refs), out_shape=jax.ShapeDty...  189 us

profile of v11, /device:TPU:1, one launch (start us, length us, event | category | flops | bytes accessed | tf_op | source)
XLA Modules:
  0.0 201.5 jit_solution(14149154472795052904)
XLA Ops:
  0.0 1.2 dynamic_slice.28
  3.2 0.7 fusion.6
  3.9 0.7 and_select_fusion.1
  4.6 0.2 convert_reduce_fusion
  4.8 0.8 fusion.5.refs_10_
  5.5 0.0 copy-start
  5.5 0.2 fusion.2
  5.7 0.0 copy-start.1
  5.8 0.6 select_reduce_fusion.refs_9_
  6.3 0.6 select_reduce_fusion.1.refs_7_
  7.0 1.3 dynamic-slice_bitcast_fusion.refs_4_
  8.3 1.6 dynamic_slice.31
  9.8 0.0 copy-done
  9.8 0.0 copy-done.1
  9.8 188.6 %shard_map.82 = bf16[16,128,512]{2,1,0:T(8,128)(2,1)} custom-call(bf16[8,128,2048]{2,1,0:T(8,128)(2,1)} %refs_0_.1, bf16[2,128,2048]{2,1,0:T(8,128)(2,1)} %bitcast.16, bf16[256,2048]{1,0:T(8,128)(2,1)} %bitcast.17, bf16[16,128,512]{2,1,0:T(8,128)(2,1)} %bitcast.18, s32[16,128]{1,0:T(8,128)} %dynamic-slice_bitcast_fusion.refs_4_, s32[16,128]{1,0:T(8,128)} %bitcast.19, ...), custom_call_target="tpu_custom_call" | custom-call | tf_op jit(solution)/shard_map/pallas_call | solution.py:667
  198.5 3.0 %copy.10 = bf16[1,2048,512]{2,1,0:T(8,128)(2,1)} copy(bf16[1,2048,512]{2,1,0:T(8,128)(2,1)} %bitcast.15) | data formatting | bytes 4194304
  (2 shorter events, 0.0 us)
Async XLA Ops:
  5.5 4.3 %copy-start = (s32[16]{0:T(128)}, s32[16]{0:T(128)S(1)}, u32[]{:S(2)}) copy-start(s32[16]{0:T(128)S(1)} %fusion.5.refs_10_) | copy-start | bytes 196
  5.7 4.1 %copy-start.1 = (s32[16]{0:T(128)}, s32[16]{0:T(128)S(1)}, u32[]{:S(2)}) copy-start(s32[16]{0:T(128)S(1)} %multiply_add_fusion.refs_8_) | copy-start | bytes 196
